TPU v7x, 512 devices: a whole 4x8x8 slice. The times are simulated.
512 devices in a mesh: ctx: 16 (over z, x_lo), ch: 32 (over x_hi, y, core).
Axes of the slice: x: 4 (x_hi: 2, x_lo: 2; x = x_hi * 2 + x_lo), y: 8, z: 8, core: 2. Of those that a mesh axis runs over, the one named last changes fastest.
Arguments:
- hidden: bfloat16 [4096, 4096], P('ctx', 'ch'), may hold values from -6 to 6
- token_ids: int32 [4096], P('ctx'), may hold values from 0 to 11
- embedding: bfloat16 [12, 4096], P(None, 'ch'), may hold values from -6 to 6
- filters: bfloat16 [16, 256], replicated, may hold values from -0.5 to 0.5
- lengths: int32 [16], replicated, may hold values from 1 to 8, as said below
- cotangent: bfloat16 [4096, 4096], P('ctx', 'ch'), may hold values from -6 to 6
Outputs:
- mixed: bfloat16 [4096, 4096], P('ctx', 'ch')
- hidden_grad: bfloat16 [4096, 4096], P('ctx', 'ch')
- filter_grad: float32 [16, 256], replicated
Inputs may be any that keep to these rules, and one draw needn't show every extreme that they name: Group g's filter keeps its first 32 * lengths[g] taps; in every draw two groups have 8 blocks and one group has 1. `token_ids`: a symbol of the vocabulary.
All inputs are finite; a program needn't handle non-finite values.
Results may differ from a plain program's by a relative error of at most 0.0051.
Values may be sent and summed in bfloat16 or wider, within the bound.
No kernel may reach another device: no remote copies, remote signals or barrier semaphores. Data moves between devices by JAX's collectives and lax.ppermute only.
A program may use at most 64 MiB of HBM per device.

v0:
```python
import math

import jax
import jax.numpy as jnp
from jax import lax
from jax.sharding import PartitionSpec as P

GW = 256
BT = 32


def padded_2(x, sides, width):
    for axis, dim in sides:
        peers, length = (lax.axis_size(axis), x.shape[dim])
        up = [(i, (i + 1) % peers) for i in range(peers - 1)]
        down = [(j, i) for i, j in up]
        last = lax.slice_in_dim(x, length - width, length, axis=dim)
        leading = lax.slice_in_dim(x, 0, width, axis=dim)
        before = lax.ppermute(last, axis, up)
        after = lax.ppermute(leading, axis, down)
        x = jnp.concatenate([before, x, after], axis=dim)
    return x


def pad_taps(taps_rows, row_count):
    zeros_side = jnp.zeros((taps_rows.shape[0], row_count), taps_rows.dtype)
    return jnp.concatenate([zeros_side, taps_rows, zeros_side], axis=1)


def toeplitz_block(padded, offset, row_count):
    start = offset * row_count + 1
    window = padded[:, start : start + 2 * row_count - 1]
    flipped = jnp.concatenate(
        [window[:, ::-1], jnp.zeros((window.shape[0], 1), window.dtype)], axis=1
    )
    tiled = jnp.tile(flipped, (1, row_count))
    cut = tiled[:, row_count - 1 : row_count - 1 + row_count * (2 * row_count - 1)]
    return cut.reshape(window.shape[0], row_count, 2 * row_count - 1)[:, :, :row_count]


def diagonal_sums(product, row_count):
    group_num = product.shape[0]
    widened = jnp.concatenate(
        [product[:, :, ::-1], jnp.zeros((group_num, row_count, row_count), product.dtype)], axis=2
    )
    flat = widened.reshape(group_num, 2 * row_count * row_count)[
        :, : row_count * (2 * row_count - 1)
    ]
    return flat.reshape(group_num, row_count, 2 * row_count - 1).sum(axis=1)


def forward_term(block, source):
    return jnp.einsum("gab,bgc->agc", block, source, preferred_element_type=jnp.float32)


def adjoint_term(block, source):
    return jnp.einsum("gba,bgc->agc", block, source, preferred_element_type=jnp.float32)


def correlate(first_rows, second_rows):
    return jnp.einsum("agc,bgc->gab", first_rows, second_rows, preferred_element_type=jnp.float32)


def own_build(block, items):
    inputs_left, grads_right, grads_here = items
    row_count = block.shape[1]
    return (
        forward_term(block, inputs_left),
        adjoint_term(block, grads_right),
        diagonal_sums(correlate(grads_here, inputs_left), row_count),
    )


def other_build(block, items):
    inputs_right, grads_left, grads_here = items
    row_count = block.shape[1]
    return (
        adjoint_term(block, inputs_right),
        forward_term(block, grads_left),
        diagonal_sums(correlate(inputs_right, grads_here), row_count),
    )


def strand_terms(padded, offset, items, build):
    row_count = items[0].shape[0]
    return build(toeplitz_block(padded, offset, row_count), items)


def add_terms(totals, terms, offset, row_count):
    start = offset * row_count + 1
    return (
        totals[0] + terms[0],
        totals[1] + terms[1],
        totals[2].at[:, start : start + 2 * row_count - 1].add(terms[2]),
    )


def folded_path(ext_inputs, ext_grads, own_pad, other_pad, shape3, reach_blocks, tap_count):
    row_count = shape3[0]
    blocks_in = ext_inputs.reshape((2 * reach_blocks + 1,) + shape3)
    blocks_grad = ext_grads.reshape((2 * reach_blocks + 1,) + shape3)
    zeros_rows = jnp.zeros(shape3, jnp.float32)
    zeros_taps = jnp.zeros((shape3[1], (reach_blocks + 2) * row_count), jnp.float32)
    own_tot = (zeros_rows, zeros_rows, zeros_taps)
    other_tot = (zeros_rows, zeros_rows, zeros_taps)
    grads_here = blocks_grad[reach_blocks]
    for offset in range(reach_blocks + 1):
        own_items = (
            blocks_in[reach_blocks - offset],
            blocks_grad[reach_blocks + offset],
            grads_here,
        )
        own_tot = add_terms(
            own_tot, strand_terms(own_pad, offset, own_items, own_build), offset, row_count
        )
        other_items = (
            blocks_in[reach_blocks + offset],
            blocks_grad[reach_blocks - offset],
            grads_here,
        )
        other_tot = add_terms(
            other_tot, strand_terms(other_pad, offset, other_items, other_build), offset, row_count
        )
    out_rows = own_tot[0] + other_tot[0]
    grad_rows = own_tot[1] + other_tot[1]
    return (
        out_rows,
        grad_rows,
        [
            own_tot[2][:, row_count : row_count + tap_count],
            other_tot[2][:, row_count : row_count + tap_count],
        ],
    )


def on_device(hidden, token_ids, embedding, filters, lengths, cotangent):
    row_count, chan_count = hidden.shape
    group_count, tap_count = filters.shape
    reach_blocks = -(-(tap_count - 1) // row_count)
    group_part = min(chan_count, GW)
    group_num = chan_count // group_part
    shape3 = (row_count, group_num, group_part)
    chan_index = lax.axis_index("ch")
    first_group = chan_index * chan_count // GW
    table_rows = embedding.astype(jnp.float32)
    looked = jnp.zeros((row_count, chan_count), jnp.float32)
    for symbol in range(embedding.shape[0]):
        looked = looked + jnp.where(
            (token_ids == symbol)[:, None], table_rows[symbol][None, :], 0.0
        )
    inputs = (hidden.astype(jnp.float32) + looked).astype(jnp.bfloat16)
    tap_mask = jnp.arange(tap_count, dtype=jnp.int32)[None, :] < (lengths * BT)[:, None]
    masked = jnp.where(tap_mask, filters, jnp.zeros_like(filters))
    own_pad = pad_taps(lax.dynamic_slice_in_dim(masked, first_group, group_num, 0), row_count)
    other_start = group_count - first_group - group_num
    other_pad = pad_taps(
        lax.dynamic_slice_in_dim(masked, other_start, group_num, 0)[::-1], row_count
    )
    ext_inputs = padded_2(inputs, (("ctx", 0),), reach_blocks * row_count)
    ext_grads = padded_2(cotangent, (("ctx", 0),), reach_blocks * row_count)
    out_rows, grad_rows, tap_parts = folded_path(
        ext_inputs, ext_grads, own_pad, other_pad, shape3, reach_blocks, tap_count
    )
    mixed = out_rows.reshape(row_count, chan_count).astype(jnp.bfloat16)
    hidden_grad = grad_rows.reshape(row_count, chan_count).astype(jnp.bfloat16)
    zeros_table = jnp.zeros((group_count, tap_count), jnp.float32)
    table = lax.dynamic_update_slice(zeros_table, tap_parts[0], (first_group, 0))
    table = table + lax.dynamic_update_slice(zeros_table, tap_parts[1][::-1], (other_start, 0))
    summed_table = lax.psum(table, ("ctx", "ch"))
    scale = 1.0 / math.sqrt(row_count * lax.axis_size("ctx") * GW)
    filter_grad = jnp.where(tap_mask, summed_table * scale, jnp.float32(0.0))
    return (mixed, hidden_grad, filter_grad)


def solution(mesh):
    placed = (P("ctx", "ch"), P("ctx"), P(None, "ch"), P(), P(), P("ctx", "ch"))
    return jax.shard_map(
        on_device,
        mesh=mesh,
        in_specs=placed,
        out_specs=(P("ctx", "ch"), P("ctx", "ch"), P()),
        check_vma=False,
    )
```

profile of v0, /device:TPU:1, one launch (start us, length us, event | category | flops | bytes accessed | tf_op | source)
XLA Modules:
  0.0 151.2 jit_solution(8839632538140957376)
XLA Ops:
  0.6 0.7 convert_element_type.28
  1.4 0.7 broadcast_compare_fusion.11
  2.1 0.6 add_convert_fusion
  2.7 1.3 collective-permute-start.1
  4.0 4.6 %collective-permute-start = (bf16[256,128]{1,0:T(8,128)(2,1)S(1)}, bf16[256,128]{1,0:T(8,128)(2,1)S(1)}, u32[]{:S(2)}, u32[]{:S(2)}) collective-permute-start(bf16[256,128]{1,0:T(8,128)(2,1)S(1)} %add_convert_fusion), channel_id=1, source_target_pairs={{0,32},{32,64},{64,96},{96,128},{128,160},{160,192},{192,224},{224... | collective-permute-start | bytes 196616 | tf_op jit(solution)/shard_map/ppermute | solution.py:19
  8.6 4.3 %collective-permute-start.3 = (bf16[256,128]{1,0:T(8,128)(2,1)S(1)}, bf16[256,128]{1,0:T(8,128)(2,1)S(1)}, u32[]{:S(2)}, u32[]{:S(2)}) collective-permute-start(bf16[256,128]{1,0:T(8,128)(2,1)S(1)} %copy-done), channel_id=1, source_target_pairs={{0,32},{32,64},{64,96},{96,128},{128,160},{160,192},{192,224},{224... | collective-permute-start | bytes 196616 | tf_op jit(solution)/shard_map/ppermute | solution.py:19
  12.9 1.3 collective-permute-start.2
  14.2 0.6 copy-done.3
  14.9 0.7 copy-done.2
  17.1 1.5 %slice_reduce_fusion.5 = bf16[130816]{0:T(1024)(128)(2,1)S(1)} fusion(bf16[1,131072]{1,0:T(2,128)(2,1)S(1)} %bitcast.105), kind=kLoop, calls=%fused_computation.19 | loop fusion | bytes 523264 | tf_op jit(solution)/shard_map/slice | solution.py:37
  18.7 0.5 reshape.306
  21.0 1.5 %slice_reduce_fusion.7 = bf16[130816]{0:T(1024)(128)(2,1)S(1)} fusion(bf16[1,131072]{1,0:T(2,128)(2,1)S(1)} %bitcast.106), kind=kLoop, calls=%fused_computation.21 | loop fusion | bytes 523264 | tf_op jit(solution)/shard_map/slice | solution.py:37
  22.5 0.5 reshape.302
  23.6 0.6 compare_reduce_fusion
  24.7 1.5 %slice_reduce_fusion.4 = bf16[130816]{0:T(1024)(128)(2,1)S(1)} fusion(bf16[1,131072]{1,0:T(2,128)(2,1)S(1)} %bitcast.107), kind=kLoop, calls=%fused_computation.18 | loop fusion | bytes 523264 | tf_op jit(solution)/shard_map/slice | solution.py:37
  27.6 0.5 copy.19
  28.1 1.4 slice_reduce_fusion.3
  29.9 0.5 copy.21
  30.5 1.4 slice_reduce_fusion.1
  32.4 0.7 broadcast_select_fusion.1
  33.0 0.7 broadcast_select_fusion
  33.7 1.5 slice_reduce_fusion.6
  35.2 0.4 reshape.308
  35.6 0.4 reshape.304
  36.9 0.5 copy.22
  37.4 1.4 slice_reduce_fusion
  40.0 0.5 copy.20
  40.6 1.4 slice_reduce_fusion.2
  43.4 105.2 %psum.7 = f32[16,256]{1,0:T(8,128)S(1)} all-reduce(f32[16,256]{1,0:T(8,128)S(1)} %add.153), channel_id=1, replica_groups=mesh['ctx'=16,'ch'=32] {'ctx','ch'}, use_global_device_ids=true, to_apply=%region_5.6 | all-reduce | flops 4096 | bytes 32768 | tf_op jit(solution)/shard_map/psum | solution.py:169
  149.0 0.7 multiply_select_fusion
  149.6 0.7 copy.12
  150.4 0.9 fusion.2
  (72 shorter events, 10.4 us)
Async XLA Ops:
  0.6 1.4 copy-start.1
  2.1 6.5 %copy-start = (bf16[256,128]{1,0:T(8,128)(2,1)S(1)}, bf16[256,128]{1,0:T(8,128)(2,1)}, u32[]{:S(2)}) copy-start(bf16[256,128]{1,0:T(8,128)(2,1)} %param.19) | copy-start | bytes 196612
  2.7 33.5 %collective-permute-start.1 = (bf16[256,128]{1,0:T(8,128)(2,1)S(1)}, bf16[256,128]{1,0:T(8,128)(2,1)S(1)}, u32[]{:S(2)}, u32[]{:S(2)}) collective-permute-start(bf16[256,128]{1,0:T(8,128)(2,1)S(1)} %add_convert_fusion), channel_id=1, source_target_pairs={{32,0},{64,32},{96,64},{128,96},{160,128},{192,160},{224,192},{256... | collective-permute-start | bytes 196616 | tf_op jit(solution)/shard_map/ppermute | solution.py:20
  4.0 35.2 %collective-permute-start = (bf16[256,128]{1,0:T(8,128)(2,1)S(1)}, bf16[256,128]{1,0:T(8,128)(2,1)S(1)}, u32[]{:S(2)}, u32[]{:S(2)}) collective-permute-start(bf16[256,128]{1,0:T(8,128)(2,1)S(1)} %add_convert_fusion), channel_id=1, source_target_pairs={{0,32},{32,64},{64,96},{96,128},{128,160},{160,192},{192,224},{224... | collective-permute-start | bytes 196616 | tf_op jit(solution)/shard_map/ppermute | solution.py:19
  8.6 140.0 %collective-permute-start.3 = (bf16[256,128]{1,0:T(8,128)(2,1)S(1)}, bf16[256,128]{1,0:T(8,128)(2,1)S(1)}, u32[]{:S(2)}, u32[]{:S(2)}) collective-permute-start(bf16[256,128]{1,0:T(8,128)(2,1)S(1)} %copy-done), channel_id=1, source_target_pairs={{0,32},{32,64},{64,96},{96,128},{128,160},{160,192},{192,224},{224... | collective-permute-start | bytes 196616 | tf_op jit(solution)/shard_map/ppermute | solution.py:19
  12.9 137.5 %collective-permute-start.2 = (bf16[256,128]{1,0:T(8,128)(2,1)S(1)}, bf16[256,128]{1,0:T(8,128)(2,1)S(1)}, u32[]{:S(2)}, u32[]{:S(2)}) collective-permute-start(bf16[256,128]{1,0:T(8,128)(2,1)S(1)} %copy-done), channel_id=1, source_target_pairs={{32,0},{64,32},{96,64},{128,96},{160,128},{192,160},{224,192},{256... | collective-permute-start | bytes 196616 | tf_op jit(solution)/shard_map/ppermute | solution.py:20
  14.2 0.7 copy-start.3
  14.9 0.7 copy-start.2
where the time goes:
time: 152 us; the launch traced here: 151 us
  blocking collectives  105 us (69%)
  local copies, waits for them, and re-layouts  25.5 us (17%)
  starting transfers between devices  11.4 us (8%)
  other arithmetic  5.19 us (3%)
  matrix products  2.77 us (2%)
    psum x1, blocking collectives, on_device(): summed_table = lax.psum(table, ('ctx', 'ch'))  105 us
    ppermute x2, starting transfers between devices, padded_2(): before = lax.ppermute(last, axis, up)  8.84 us
    unnamed x35, local copies, waits for them, and re-layouts  8.22 us
    slice x4, local copies, waits for them, and re-layouts, toeplitz_block(): tiled[:, row_count - 1:row_count - 1 + row_count * (2 * row_count - 1)]  6.09 us
    slice x4, local copies, waits for them, and re-layouts, diagonal_sums(): widened.reshape(group_num, 2 * row_count * row_count)  5.44 us
  transfers between devices with their start and end apart: 4, of which 0 were waited for; matrix products, arithmetic and copies ran while one was open for 19% of the time, Pallas kernels for 0%

commit v1 on v0

v1 whole, which is shorter than its diff:
```python
import math

import jax
import jax.numpy as jnp
from jax import lax
from jax.experimental import pallas as pl
from jax.experimental.pallas import tpu as pltpu
from jax.sharding import Mesh, PartitionSpec as P

GW = 256
BT = 32
ROWS = 256
CHANS = 128
TAPS = 256
GROUPS = 16
PARTS = (("z", 8), ("x_lo", 2), ("x_hi", 2), ("y", 8), ("core", 2))
CTX = ("z", "x_lo")
GROUP = ("x_hi", "y")
SUMMED = ("z", "x_lo", "core")
CTX_SIZE = 16
SUMMED_SIZE = 32

VMEM = pl.BlockSpec(memory_space=pltpu.VMEM)
SMEM = pl.BlockSpec(memory_space=pltpu.SMEM)


def dot(a, b, contract):
    return lax.dot_general(a, b, (contract, ((), ())), preferred_element_type=jnp.float32)


def cost(flops, moved):
    return pl.CostEstimate(flops=flops, bytes_accessed=moved, transcendentals=0)


ROOM = pltpu.CompilerParams(vmem_limit_bytes=16 * 1024 * 1024)


def iota(shape, dim):
    return lax.broadcasted_iota(jnp.int32, shape, dim)


def inputs_kernel(hidden, ids, table, cotangent, both):
    symbols = table.shape[0]
    shape = (symbols, ROWS)
    ids_row = jnp.broadcast_to(ids[...].reshape(1, ROWS), shape)
    onehot = jnp.where(iota(shape, 0) == ids_row, 1.0, 0.0)
    looked = dot(onehot, table[...].astype(jnp.float32), ((0,), (0,)))
    both[0] = (hidden[...].astype(jnp.float32) + looked).astype(jnp.bfloat16)
    both[1] = cotangent[...]


def lag_sums(product):
    half = ROWS // 2
    while half >= 8:
        product = product[:half] + pltpu.roll(product[half:], TAPS - half, 1)
        half //= 2
    row = iota(product.shape, 0)
    for step in (4, 2, 1):
        product = jnp.where((row & step) != 0, pltpu.roll(product, TAPS - step, 1), product)
    return jnp.sum(product, axis=0, keepdims=True)


def correlate_kernel(both, left, out):
    shape = (ROWS, ROWS)
    here = iota(shape, 1) >= iota(shape, 0)
    lane = ((1,), (1,))
    sums = []
    for first, second in ((0, 1), (1, 0)):
        fixed = both[second]
        near = dot(both[first], fixed, lane)
        far = dot(left[first], fixed, lane)
        sums.append(lag_sums(jnp.where(here, near, far)))
    half = TAPS // 2
    pieces = [sums[0][:, :half], sums[0][:, half:], sums[1][:, :half], sums[1][:, half:]]
    row = iota((4, half), 0)
    packed = jnp.where(row < 2, jnp.where(row == 0, pieces[0], pieces[1]),
                       jnp.where(row == 2, pieces[2], pieces[3]))
    for peer in range(out.shape[0]):
        out[peer] = packed


def sum_kernel(parts, out):
    total = jnp.sum(parts[...], axis=0)
    for peer in range(out.shape[0]):
        out[peer] = total


def finish_kernel(parts, factor, out):
    half = TAPS // 2
    for group in range(GROUPS):
        own = parts[group]
        other = parts[GROUPS - 1 - group]
        out[group : group + 1, :half] = own[0:1] + other[2:3]
        out[group : group + 1, half:] = own[1:2] + other[3:4]
    scaled = factor[...]
    out[...] = jnp.where(scaled != 0.0, out[...] * scaled, 0.0)


def outputs_kernel(both, left, right, filters, lengths, mixed, grad, factor):
    taps_shape = (GROUPS, TAPS)
    group_row = iota(taps_shape, 0)
    tap_lane = iota(taps_shape, 1)
    reach = jnp.zeros(taps_shape, jnp.int32)
    for group in range(GROUPS):
        reach = jnp.where(group_row == group, lengths[group] * BT, reach)
    kept = tap_lane < reach
    scale = 1.0 / math.sqrt(ROWS * CTX_SIZE * GW)
    factor[...] = jnp.where(kept, scale, 0.0)
    taps = jnp.where(kept, filters[...].astype(jnp.float32), 0.0)
    mine = lax.axis_index("x_hi") * 8 + lax.axis_index("y")

    def circulant(index):
        row = jnp.sum(jnp.where(group_row == index, taps, 0.0), axis=0, keepdims=True)
        spread = pltpu.roll(jnp.broadcast_to(row, (ROWS, TAPS)), 0, 1, stride=1, stride_axis=0)
        return row[:, :1], spread, spread.T

    own_first, own, own_t = circulant(mine)
    other_first, other, other_t = circulant(GROUPS - 1 - mine)
    shape = (ROWS, ROWS)
    row, lane = iota(shape, 0), iota(shape, 1)
    below = row > lane
    above = row < lane

    def matrix(mask, yes, no):
        return jnp.where(mask, yes, no).astype(jnp.bfloat16)

    plain = ((1,), (0,))
    inputs, cotangent = both[0], both[1]
    total = dot(matrix(below, own_t, other), inputs, plain)
    total += dot(matrix(above, own_t, 0.0), left[0], plain)
    total += dot(matrix(below, other, 0.0), right[0], plain)
    mixed[...] = (total + own_first * inputs.astype(jnp.float32)).astype(jnp.bfloat16)
    total = dot(matrix(below, other_t, own), cotangent, plain)
    total += dot(matrix(below, own, 0.0), right[1], plain)
    total += dot(matrix(above, other_t, 0.0), left[1], plain)
    grad[...] = (total + other_first * cotangent.astype(jnp.float32)).astype(jnp.bfloat16)


def on_device(hidden, token_ids, embedding, filters, lengths, cotangent):
    shape = jax.ShapeDtypeStruct
    half = TAPS // 2
    both = pl.pallas_call(
        inputs_kernel,
        out_shape=shape((2, ROWS, CHANS), jnp.bfloat16),
        in_specs=[VMEM] * 4,
        out_specs=VMEM,
        cost_estimate=cost(2 * 16 * ROWS * CHANS, 1 << 18),
    )(hidden, token_ids, embedding, cotangent)
    up = [(i, i + 1) for i in range(CTX_SIZE - 1)]
    left = lax.ppermute(both, CTX, up)
    right = lax.ppermute(both, CTX, [(j, i) for i, j in up])
    sums = pl.pallas_call(
        correlate_kernel,
        out_shape=shape((SUMMED_SIZE, 4, half), jnp.float32),
        in_specs=[VMEM] * 2,
        out_specs=VMEM,
        cost_estimate=cost(8 * ROWS * ROWS * CHANS, 1 << 18),
        compiler_params=ROOM,
    )(both, left)
    sums = lax.all_to_all(sums, SUMMED, 0, 0)
    sums = pl.pallas_call(
        sum_kernel,
        out_shape=shape((GROUPS, 4, half), jnp.float32),
        in_specs=[VMEM],
        out_specs=VMEM,
        cost_estimate=cost(1 << 16, 1 << 17),
        compiler_params=ROOM,
    )(sums)
    sums = lax.all_to_all(sums, GROUP, 0, 0)
    block = shape((ROWS, CHANS), jnp.bfloat16)
    mixed, hidden_grad, factor = pl.pallas_call(
        outputs_kernel,
        out_shape=(block, block, shape((GROUPS, TAPS), jnp.float32)),
        in_specs=[VMEM] * 4 + [SMEM],
        out_specs=(VMEM,) * 3,
        cost_estimate=cost(12 * ROWS * ROWS * CHANS, 1 << 19),
        compiler_params=ROOM,
    )(both, left, right, filters, lengths)
    filter_grad = pl.pallas_call(
        finish_kernel,
        out_shape=shape((GROUPS, TAPS), jnp.float32),
        in_specs=[VMEM] * 2,
        out_specs=VMEM,
        cost_estimate=cost(1 << 14, 1 << 16),
        compiler_params=ROOM,
    )(sums, factor)
    return mixed, hidden_grad, filter_grad


def solution(mesh):
    names = tuple(name for name, _ in PARTS)
    fine = Mesh(mesh.devices.reshape([size for _, size in PARTS]), names)
    ctx, ch = names[:2], names[2:]
    placed = (P(ctx, ch), P(ctx), P(None, ch), P(), P(), P(ctx, ch))
    return jax.shard_map(
        on_device,
        mesh=fine,
        in_specs=placed,
        out_specs=(P(ctx, ch), P(ctx, ch), P()),
        check_vma=False,
    )
```

time: 152 us -> 54.5 us (0.36)
  blocking collectives: 105 us -> 0 us
  local copies, waits for them, and re-layouts: 25.5 us -> 0.91 us
  starting transfers between devices: 11.4 us -> 29.9 us
  waiting for transfers between devices: 0.01 us -> 16.4 us
  Pallas kernels: 0 us -> 6.17 us
  other arithmetic: 5.19 us -> 0 us
  matrix products: 2.77 us -> 0 us
    psum x1 -> x0, blocking collectives: 105 us -> none  [on_device(): summed_table = lax.psum(table, ('ctx', 'ch'))]
    all_to_all x0 -> x2, starting transfers between devices: none -> 24.7 us  [the longest x1 15.2 us: on_device(): sums = lax.all_to_all(sums, SUMMED, 0, 0)]
    all_to_all x0 -> x2, waiting for transfers between devices: none -> 14.1 us  [the longest x1 7.13 us: on_device(): sums = lax.all_to_all(sums, GROUP, 0, 0)]
    slice x11 -> x0, local copies, waits for them, and re-layouts: 11.7 us -> none  [the longest x4 6.09 us: toeplitz_block(): tiled[:, row_count - 1:row_count - 1 + row_count * (2 * row_count - 1)]]
    unnamed x35 -> x8, local copies, waits for them, and re-layouts: 8.22 us -> 0.91 us
    ppermute x4 -> x2, starting transfers between devices: 11.4 us -> 5.23 us  [the longest x1 3.94 us: on_device(): left = lax.ppermute(both, CTX, up)]
    pallas_call x0 -> x5, Pallas kernels: none -> 6.17 us  [the longest x1 1.77 us: on_device(): pl.pallas_call(inputs_kernel, out_shape=shape((2, ROWS, CHANS), jnp.bfloa...]
    reshape x8 -> x0, local copies, waits for them, and re-layouts: 3.33 us -> none  [the longest x4 1.79 us: toeplitz_block(): cut.reshape(window.shape[0], row_count, 2 * row_count - 1)[:, :, :row_count]]
  transfers between devices with their start and end apart: 4 -> 4, of which waited for: 0 -> 3; matrix products, arithmetic and copies ran while one was open for 19% -> 0% of each run, Pallas kernels for 0% -> 4%
where the time goes in v1:
time: 54.5 us; the launch traced here: 54.1 us
  starting transfers between devices  29.9 us (55%)
  waiting for transfers between devices  16.4 us (30%)
  Pallas kernels  6.17 us (11%)
  local copies, waits for them, and re-layouts  0.91 us (2%)
  between operations  0.7 us (1%)
    all_to_all x1, starting transfers between devices, on_device(): sums = lax.all_to_all(sums, SUMMED, 0, 0)  15.2 us
    all_to_all x1, starting transfers between devices, on_device(): sums = lax.all_to_all(sums, GROUP, 0, 0)  9.52 us
    all_to_all x1, waiting for transfers between devices, on_device(): sums = lax.all_to_all(sums, GROUP, 0, 0)  7.13 us
    all_to_all x1, waiting for transfers between devices, on_device(): sums = lax.all_to_all(sums, SUMMED, 0, 0)  7.02 us
    ppermute x1, starting transfers between devices, on_device(): left = lax.ppermute(both, CTX, up)  3.94 us
    ppermute x1, waiting for transfers between devices, on_device(): left = lax.ppermute(both, CTX, up)  2.24 us
    pallas_call x1, Pallas kernels, on_device(): pl.pallas_call(inputs_kernel, out_shape=shape((2, ROWS, CHANS), jnp.bfloa...  1.77 us
    pallas_call x1, Pallas kernels, on_device(): pl.pallas_call(outputs_kernel, out_shape=(block, block, shape((GROUPS, TA...  1.69 us
  transfers between devices with their start and end apart: 4, of which 3 were waited for; matrix products, arithmetic and copies ran while one was open for 0% of the time, Pallas kernels for 4%

profile of v1, /device:TPU:1, one launch (start us, length us, event | category | flops | bytes accessed | tf_op | source)
XLA Modules:
  0.0 54.1 jit_solution(10408952477202718411)
XLA Ops:
  0.6 1.8 %shard_map.85.both = bf16[2,256,128]{2,1,0:T(8,128)(2,1)} custom-call(bf16[256,128]{1,0:T(8,128)(2,1)} %hidden.1, s32[256]{0:T(256)} %ids.1, bf16[12,128]{1,0:T(8,128)(2,1)} %table.1, bf16[256,128]{1,0:T(8,128)(2,1)} %cotangent.1), custom_call_target="tpu_custom_call" | custom-call | flops 1048576 | bytes 262144 | tf_op jit(solution)/shard_map/pallas_call | solution.py:142
  2.4 3.9 %collective-permute-start = (bf16[2,256,128]{2,1,0:T(8,128)(2,1)}, bf16[2,256,128]{2,1,0:T(8,128)(2,1)S(1)}, u32[]{:S(2)}, u32[]{:S(2)}) collective-permute-start(bf16[2,256,128]{2,1,0:T(8,128)(2,1)} %shard_map.85.both), channel_id=1, source_target_pairs={{0,32},{32,64},{64,96},{96,128},{128,160},{160,192},{192,224},{224... | collective-permute-start | bytes 393224 | tf_op jit(solution)/shard_map/ppermute | solution.py:150
  6.3 2.2 %collective-permute-done.left = bf16[2,256,128]{2,1,0:T(8,128)(2,1)S(1)} collective-permute-done((bf16[2,256,128]{2,1,0:T(8,128)(2,1)}, bf16[2,256,128]{2,1,0:T(8,128)(2,1)S(1)}, u32[]{:S(2)}, u32[]{:S(2)}) %collective-permute-start) | collective-permute-done | bytes 131104 | tf_op jit(solution)/shard_map/ppermute | solution.py:150
  8.6 0.0 copy-start
  8.6 0.9 %copy-done = bf16[2,256,128]{2,1,0:T(8,128)(2,1)S(1)} copy-done((bf16[2,256,128]{2,1,0:T(8,128)(2,1)S(1)}, bf16[2,256,128]{2,1,0:T(8,128)(2,1)}, u32[]{:S(2)}) %copy-start) | copy-done | bytes 131096
  9.5 0.0 copy-start.1
  9.5 1.4 %shard_map.87 = f32[32,4,128]{2,1,0:T(4,128)} custom-call(bf16[2,256,128]{2,1,0:T(8,128)(2,1)S(1)} %copy-done, bf16[2,256,128]{2,1,0:T(8,128)(2,1)S(1)} %collective-permute-done.left), custom_call_target="tpu_custom_call" | custom-call | flops 67108864 | bytes 262144 | tf_op jit(solution)/shard_map/pallas_call | solution.py:152
  10.9 15.2 %all-to-all-start = ((f32[32,4,128]{2,1,0:T(4,128)}), f32[32,4,128]{2,1,0:T(4,128)S(1)}, u32[]{:S(2)}, u32[]{:S(2)}) async-start(f32[32,4,128]{2,1,0:T(4,128)} %shard_map.87), calls=%async_computation | async-start | bytes 131072 | tf_op jit(solution)/shard_map/all_to_all | solution.py:160
  26.1 0.0 copy-done.1
  26.1 1.3 %collective-permute-start.1 = (bf16[2,256,128]{2,1,0:T(8,128)(2,1)S(1)}, bf16[2,256,128]{2,1,0:T(8,128)(2,1)S(1)}, u32[]{:S(2)}, u32[]{:S(2)}) collective-permute-start(bf16[2,256,128]{2,1,0:T(8,128)(2,1)S(1)} %copy-done.1), channel_id=1, source_target_pairs={{32,0},{64,32},{96,64},{128,96},{160,128},{192,160},{224,192},{256... | collective-permute-start | bytes 393224 | tf_op jit(solution)/shard_map/ppermute | solution.py:151
  27.4 7.0 %all-to-all-done.parts = f32[32,4,128]{2,1,0:T(4,128)S(1)} async-done(((f32[32,4,128]{2,1,0:T(4,128)}), f32[32,4,128]{2,1,0:T(4,128)S(1)}, u32[]{:S(2)}, u32[]{:S(2)}) %all-to-all-start) | async-done | bytes 65568 | tf_op jit(solution)/shard_map/all_to_all | solution.py:160
  34.4 0.7 %shard_map.88 = f32[16,4,128]{2,1,0:T(4,128)} custom-call(f32[32,4,128]{2,1,0:T(4,128)S(1)} %all-to-all-done.parts), custom_call_target="tpu_custom_call" | custom-call | flops 65536 | bytes 131072 | tf_op jit(solution)/shard_map/pallas_call | solution.py:161
  35.1 0.0 copy-start.2
  35.1 0.0 copy-start.3
  35.1 9.5 %all-to-all-start.1 = ((f32[16,4,128]{2,1,0:T(4,128)}), f32[16,4,128]{2,1,0:T(4,128)S(1)}, u32[]{:S(2)}, u32[]{:S(2)}) async-start(f32[16,4,128]{2,1,0:T(4,128)} %shard_map.88), calls=%async_computation.1 | async-start | bytes 65536 | tf_op jit(solution)/shard_map/all_to_all | solution.py:169
  44.6 0.0 collective-permute-done.1.right
  44.6 0.0 copy-done.2
  44.7 0.0 copy-done.3
  44.7 1.7 %shard_map.86 = (bf16[256,128]{1,0:T(8,128)(2,1)}, bf16[256,128]{1,0:T(8,128)(2,1)}, f32[16,256]{1,0:T(8,128)S(1)}) custom-call(bf16[2,256,128]{2,1,0:T(8,128)(2,1)S(1)} %copy-done.1, bf16[2,256,128]{2,1,0:T(8,128)(2,1)S(1)} %collective-permute-done.left, bf16[2,256,128]{2,1,0:T(8,128)(2,1)S(1)} %collective-permute-done.1.right, ...), custom_call_target="tpu_custom_call" | custom-call | flops 100663296 | bytes 524288 | tf_op jit(solution)/shard_map/pallas_call | solution.py:171
  46.4 7.1 %all-to-all-done.1.parts = f32[16,4,128]{2,1,0:T(4,128)S(1)} async-done(((f32[16,4,128]{2,1,0:T(4,128)}), f32[16,4,128]{2,1,0:T(4,128)S(1)}, u32[]{:S(2)}, u32[]{:S(2)}) %all-to-all-start.1) | async-done | bytes 32800 | tf_op jit(solution)/shard_map/all_to_all | solution.py:169
  53.5 0.6 %shard_map.89 = f32[16,256]{1,0:T(8,128)} custom-call(f32[16,4,128]{2,1,0:T(4,128)S(1)} %all-to-all-done.1.parts, f32[16,256]{1,0:T(8,128)S(1)} %get-tuple-element.8.factor), custom_call_target="tpu_custom_call" | custom-call | flops 16384 | bytes 65536 | tf_op jit(solution)/shard_map/pallas_call | solution.py:179
Async XLA Ops:
  2.4 6.2 %collective-permute-start = (bf16[2,256,128]{2,1,0:T(8,128)(2,1)}, bf16[2,256,128]{2,1,0:T(8,128)(2,1)S(1)}, u32[]{:S(2)}, u32[]{:S(2)}) collective-permute-start(bf16[2,256,128]{2,1,0:T(8,128)(2,1)} %shard_map.85.both), channel_id=1, source_target_pairs={{0,32},{32,64},{64,96},{96,128},{128,160},{160,192},{192,224},{224... | collective-permute-start | bytes 393224 | tf_op jit(solution)/shard_map/ppermute | solution.py:150
  8.6 0.9 %copy-start = (bf16[2,256,128]{2,1,0:T(8,128)(2,1)S(1)}, bf16[2,256,128]{2,1,0:T(8,128)(2,1)}, u32[]{:S(2)}) copy-start(bf16[2,256,128]{2,1,0:T(8,128)(2,1)} %shard_map.85.both) | copy-start | bytes 393220
  9.5 16.6 %copy-start.1 = (bf16[2,256,128]{2,1,0:T(8,128)(2,1)S(1)}, bf16[2,256,128]{2,1,0:T(8,128)(2,1)}, u32[]{:S(2)}) copy-start(bf16[2,256,128]{2,1,0:T(8,128)(2,1)} %shard_map.85.both) | copy-start | bytes 393220
  10.9 23.5 %all-to-all-start = ((f32[32,4,128]{2,1,0:T(4,128)}), f32[32,4,128]{2,1,0:T(4,128)S(1)}, u32[]{:S(2)}, u32[]{:S(2)}) async-start(f32[32,4,128]{2,1,0:T(4,128)} %shard_map.87), calls=%async_computation | async-start | bytes 131072 | tf_op jit(solution)/shard_map/all_to_all | solution.py:160
  26.1 18.5 %collective-permute-start.1 = (bf16[2,256,128]{2,1,0:T(8,128)(2,1)S(1)}, bf16[2,256,128]{2,1,0:T(8,128)(2,1)S(1)}, u32[]{:S(2)}, u32[]{:S(2)}) collective-permute-start(bf16[2,256,128]{2,1,0:T(8,128)(2,1)S(1)} %copy-done.1), channel_id=1, source_target_pairs={{32,0},{64,32},{96,64},{128,96},{160,128},{192,160},{224,192},{256... | collective-permute-start | bytes 393224 | tf_op jit(solution)/shard_map/ppermute | solution.py:151
  35.1 9.5 %copy-start.2 = (bf16[16,256]{1,0:T(8,128)(2,1)S(1)}, bf16[16,256]{1,0:T(8,128)(2,1)}, u32[]{:S(2)}) copy-start(bf16[16,256]{1,0:T(8,128)(2,1)} %filters.1) | copy-start | bytes 24580
  35.1 9.6 %copy-start.3 = (s32[16]{0:T(128)S(1)}, s32[16]{0:T(128)}, u32[]{:S(2)}) copy-start(s32[16]{0:T(128)} %lengths.1) | copy-start | bytes 196
  35.1 18.4 %all-to-all-start.1 = ((f32[16,4,128]{2,1,0:T(4,128)}), f32[16,4,128]{2,1,0:T(4,128)S(1)}, u32[]{:S(2)}, u32[]{:S(2)}) async-start(f32[16,4,128]{2,1,0:T(4,128)} %shard_map.88), calls=%async_computation.1 | async-start | bytes 65536 | tf_op jit(solution)/shard_map/all_to_all | solution.py:169

commit v2 on v1

--- a/solution.py
+++ b/solution.py
@@ -39,14 +39,13 @@
     return lax.broadcasted_iota(jnp.int32, shape, dim)
 
 
-def inputs_kernel(hidden, ids, table, cotangent, both):
+def inputs_kernel(hidden, ids, table, inputs):
     symbols = table.shape[0]
     shape = (symbols, ROWS)
     ids_row = jnp.broadcast_to(ids[...].reshape(1, ROWS), shape)
     onehot = jnp.where(iota(shape, 0) == ids_row, 1.0, 0.0)
     looked = dot(onehot, table[...].astype(jnp.float32), ((0,), (0,)))
-    both[0] = (hidden[...].astype(jnp.float32) + looked).astype(jnp.bfloat16)
-    both[1] = cotangent[...]
+    inputs[...] = (hidden[...].astype(jnp.float32) + looked).astype(jnp.bfloat16)
 
 
 def lag_sums(product):
@@ -60,16 +59,14 @@
     return jnp.sum(product, axis=0, keepdims=True)
 
 
-def correlate_kernel(both, left, out):
+def correlate_kernel(inputs, cotangent, left, right, out):
     shape = (ROWS, ROWS)
     here = iota(shape, 1) >= iota(shape, 0)
     lane = ((1,), (1,))
-    sums = []
-    for first, second in ((0, 1), (1, 0)):
-        fixed = both[second]
-        near = dot(both[first], fixed, lane)
-        far = dot(left[first], fixed, lane)
-        sums.append(lag_sums(jnp.where(here, near, far)))
+    source, grads = inputs[...], cotangent[...]
+    own = jnp.where(here, dot(source, grads, lane), dot(source, right[...], lane))
+    other = jnp.where(here, dot(grads, source, lane), dot(left[...], source, lane))
+    sums = [lag_sums(own), lag_sums(other)]
     half = TAPS // 2
     pieces = [sums[0][:, :half], sums[0][:, half:], sums[1][:, :half], sums[1][:, half:]]
     row = iota((4, half), 0)
@@ -96,7 +93,7 @@
     out[...] = jnp.where(scaled != 0.0, out[...] * scaled, 0.0)
 
 
-def outputs_kernel(both, left, right, filters, lengths, mixed, grad, factor):
+def outputs_kernel(inputs, cotangent, in_left, in_right, ct_left, ct_right, filters, lengths, mixed, grad, factor):
     taps_shape = (GROUPS, TAPS)
     group_row = iota(taps_shape, 0)
     tap_lane = iota(taps_shape, 1)
@@ -125,38 +122,44 @@
         return jnp.where(mask, yes, no).astype(jnp.bfloat16)
 
     plain = ((1,), (0,))
-    inputs, cotangent = both[0], both[1]
-    total = dot(matrix(below, own_t, other), inputs, plain)
-    total += dot(matrix(above, own_t, 0.0), left[0], plain)
-    total += dot(matrix(below, other, 0.0), right[0], plain)
-    mixed[...] = (total + own_first * inputs.astype(jnp.float32)).astype(jnp.bfloat16)
-    total = dot(matrix(below, other_t, own), cotangent, plain)
-    total += dot(matrix(below, own, 0.0), right[1], plain)
-    total += dot(matrix(above, other_t, 0.0), left[1], plain)
-    grad[...] = (total + other_first * cotangent.astype(jnp.float32)).astype(jnp.bfloat16)
+    source, grads = inputs[...], cotangent[...]
+    total = dot(matrix(below, own_t, other), source, plain)
+    total += dot(matrix(above, own_t, 0.0), in_left[...], plain)
+    total += dot(matrix(below, other, 0.0), in_right[...], plain)
+    mixed[...] = (total + own_first * source.astype(jnp.float32)).astype(jnp.bfloat16)
+    total = dot(matrix(below, other_t, own), grads, plain)
+    total += dot(matrix(below, own, 0.0), ct_right[...], plain)
+    total += dot(matrix(above, other_t, 0.0), ct_left[...], plain)
+    grad[...] = (total + other_first * grads.astype(jnp.float32)).astype(jnp.bfloat16)
 
 
 def on_device(hidden, token_ids, embedding, filters, lengths, cotangent):
     shape = jax.ShapeDtypeStruct
     half = TAPS // 2
-    both = pl.pallas_call(
+    up = [(i, i + 1) for i in range(CTX_SIZE - 1)]
+    down = [(j, i) for i, j in up]
+    ct_left = lax.ppermute(cotangent, CTX, up)
+    ct_right = lax.ppermute(cotangent, CTX, down)
+    block = shape((ROWS, CHANS), jnp.bfloat16)
+    inputs = pl.pallas_call(
         inputs_kernel,
-        out_shape=shape((2, ROWS, CHANS), jnp.bfloat16),
-        in_specs=[VMEM] * 4,
+        out_shape=block,
+        in_specs=[VMEM] * 3,
         out_specs=VMEM,
         cost_estimate=cost(2 * 16 * ROWS * CHANS, 1 << 18),
-    )(hidden, token_ids, embedding, cotangent)
-    up = [(i, i + 1) for i in range(CTX_SIZE - 1)]
-    left = lax.ppermute(both, CTX, up)
-    right = lax.ppermute(both, CTX, [(j, i) for i, j in up])
+        compiler_params=ROOM,
+    )(hidden, token_ids, embedding)
     sums = pl.pallas_call(
         correlate_kernel,
         out_shape=shape((SUMMED_SIZE, 4, half), jnp.float32),
-        in_specs=[VMEM] * 2,
+        in_specs=[VMEM] * 4,
         out_specs=VMEM,
         cost_estimate=cost(8 * ROWS * ROWS * CHANS, 1 << 18),
         compiler_params=ROOM,
-    )(both, left)
+    )(inputs, cotangent, ct_left, ct_right)
+    sums, late_inputs = lax.optimization_barrier((sums, inputs))
+    in_left = lax.ppermute(late_inputs, CTX, up)
+    in_right = lax.ppermute(late_inputs, CTX, down)
     sums = lax.all_to_all(sums, SUMMED, 0, 0)
     sums = pl.pallas_call(
         sum_kernel,
@@ -167,15 +170,14 @@
         compiler_params=ROOM,
     )(sums)
     sums = lax.all_to_all(sums, GROUP, 0, 0)
-    block = shape((ROWS, CHANS), jnp.bfloat16)
     mixed, hidden_grad, factor = pl.pallas_call(
         outputs_kernel,
         out_shape=(block, block, shape((GROUPS, TAPS), jnp.float32)),
-        in_specs=[VMEM] * 4 + [SMEM],
+        in_specs=[VMEM] * 7 + [SMEM],
         out_specs=(VMEM,) * 3,
         cost_estimate=cost(12 * ROWS * ROWS * CHANS, 1 << 19),
         compiler_params=ROOM,
-    )(both, left, right, filters, lengths)
+    )(inputs, cotangent, in_left, in_right, ct_left, ct_right, filters, lengths)
     filter_grad = pl.pallas_call(
         finish_kernel,
         out_shape=shape((GROUPS, TAPS), jnp.float32),

time: 54.5 us -> 53.3 us (0.978)
  waiting for transfers between devices: 16.4 us -> 10.2 us
  starting transfers between devices: 29.9 us -> 35.1 us
  Pallas kernels: 6.17 us -> 4.62 us
  local copies, waits for them, and re-layouts: 0.91 us -> 2.21 us
    ppermute x2 -> x4, starting transfers between devices: 5.23 us -> 11.3 us  [the longest x1 4.58 us: on_device(): ct_left = lax.ppermute(cotangent, CTX, up)]
    all_to_all x1, waiting for transfers between devices: 7.02 us -> 3.03 us  [on_device(): sums = lax.all_to_all(sums, SUMMED, 0, 0)]
    ppermute x2 -> x4, waiting for transfers between devices: 2.24 us -> 0.01 us  [the longest x1 0.01 us: on_device(): in_left = lax.ppermute(late_inputs, CTX, up)]
    pallas_call x1, Pallas kernels: 1.77 us -> 0.22 us  [on_device(): pl.pallas_call(inputs_kernel, out_shape=block, in_specs=[VMEM] * 3, out_s...]
    unnamed x8 -> x12, local copies, waits for them, and re-layouts: 0.91 us -> 2.21 us
    all_to_all x1, starting transfers between devices: 15.2 us -> 14.6 us  [on_device(): sums = lax.all_to_all(sums, SUMMED, 0, 0)]
  transfers between devices with their start and end apart: 4 -> 6, of which waited for: 3 -> 2; matrix products, arithmetic and copies ran while one was open for 0% -> 0% of each run, Pallas kernels for 4% -> 5%
where the time goes in v2:
time: 53.3 us; the launch traced here: 52.8 us
  starting transfers between devices  35.1 us (66%)
  waiting for transfers between devices  10.2 us (19%)
  Pallas kernels  4.62 us (9%)
  local copies, waits for them, and re-layouts  2.21 us (4%)
  between operations  0.75 us (1%)
    all_to_all x1, starting transfers between devices, on_device(): sums = lax.all_to_all(sums, SUMMED, 0, 0)  14.6 us
    all_to_all x1, starting transfers between devices, on_device(): sums = lax.all_to_all(sums, GROUP, 0, 0)  9.22 us
    all_to_all x1, waiting for transfers between devices, on_device(): sums = lax.all_to_all(sums, GROUP, 0, 0)  7.12 us
    ppermute x1, starting transfers between devices, on_device(): ct_left = lax.ppermute(cotangent, CTX, up)  4.58 us
    ppermute x1, starting transfers between devices, on_device(): in_left = lax.ppermute(late_inputs, CTX, up)  3.99 us
    all_to_all x1, waiting for transfers between devices, on_device(): sums = lax.all_to_all(sums, SUMMED, 0, 0)  3.03 us
    unnamed x12, local copies, waits for them, and re-layouts  2.21 us
    pallas_call x1, Pallas kernels, on_device(): pl.pallas_call(outputs_kernel, out_shape=(block, block, shape((GROUPS, TA...  1.69 us
  transfers between devices with their start and end apart: 6, of which 2 were waited for; matrix products, arithmetic and copies ran while one was open for 0% of the time, Pallas kernels for 5%

profile of v2, /device:TPU:1, one launch (start us, length us, event | category | flops | bytes accessed | tf_op | source)
XLA Modules:
  0.0 52.8 jit_solution(7768307886266388851)
XLA Ops:
  0.6 0.0 copy-start
  0.6 1.4 %collective-permute-start.1 = (bf16[256,128]{1,0:T(8,128)(2,1)}, bf16[256,128]{1,0:T(8,128)(2,1)S(1)}, u32[]{:S(2)}, u32[]{:S(2)}) collective-permute-start(bf16[256,128]{1,0:T(8,128)(2,1)} %cotangent.3), channel_id=1, source_target_pairs={{32,0},{64,32},{96,64},{128,96},{160,128},{192,160},{224,192},{256... | collective-permute-start | bytes 196616 | tf_op jit(solution)/shard_map/ppermute | solution.py:142
  2.1 4.6 %collective-permute-start = (bf16[256,128]{1,0:T(8,128)(2,1)}, bf16[256,128]{1,0:T(8,128)(2,1)S(1)}, u32[]{:S(2)}, u32[]{:S(2)}) collective-permute-start(bf16[256,128]{1,0:T(8,128)(2,1)} %cotangent.3), channel_id=1, source_target_pairs={{0,32},{32,64},{64,96},{96,128},{128,160},{160,192},{192,224},{224... | collective-permute-start | bytes 196616 | tf_op jit(solution)/shard_map/ppermute | solution.py:141
  6.7 0.0 copy-start.1
  6.7 0.8 %copy-done.1 = bf16[256,128]{1,0:T(8,128)(2,1)S(1)} copy-done((bf16[256,128]{1,0:T(8,128)(2,1)S(1)}, bf16[256,128]{1,0:T(8,128)(2,1)}, u32[]{:S(2)}) %copy-start.1) | copy-done | bytes 65560
  7.5 0.0 copy-start.3
  7.5 0.7 %copy-done.3 = bf16[12,128]{1,0:T(8,128)(2,1)S(1)} copy-done((bf16[12,128]{1,0:T(8,128)(2,1)S(1)}, bf16[12,128]{1,0:T(8,128)(2,1)}, u32[]{:S(2)}) %copy-start.3) | copy-done | bytes 3096
  8.2 0.0 copy-start.4
  8.2 0.7 %copy-done.4 = s32[256]{0:T(256)S(1)} copy-done((s32[256]{0:T(256)S(1)}, s32[256]{0:T(256)}, u32[]{:S(2)}) %copy-start.4) | copy-done | bytes 1048
  8.9 0.2 shard_map.85.inputs
  9.1 0.0 collective-permute-done.1.right.ct_right
  9.1 0.0 collective-permute-done.left.ct_left
  9.1 0.0 copy-done
  9.1 1.4 %shard_map.86 = f32[32,4,128]{2,1,0:T(4,128)} custom-call(bf16[256,128]{1,0:T(8,128)(2,1)S(1)} %shard_map.85.inputs, bf16[256,128]{1,0:T(8,128)(2,1)S(1)} %copy-done, bf16[256,128]{1,0:T(8,128)(2,1)S(1)} %collective-permute-done.left.ct_left, bf16[256,128]{1,0:T(8,128)(2,1)S(1)} %collective-permute-done.1.right.ct_right), custom_call_target="tpu_custom_call" | custom-call | flops 67108864 | bytes 262144 | tf_op jit(solution)/shard_map/pallas_call | solution.py:152
  10.5 14.6 %all-to-all-start = ((f32[32,4,128]{2,1,0:T(4,128)}), f32[32,4,128]{2,1,0:T(4,128)S(1)}, u32[]{:S(2)}, u32[]{:S(2)}) async-start(f32[32,4,128]{2,1,0:T(4,128)} %shard_map.86), calls=%async_computation | async-start | bytes 131072 | tf_op jit(solution)/shard_map/all_to_all | solution.py:163
  25.1 1.3 %collective-permute-start.3 = (bf16[256,128]{1,0:T(8,128)(2,1)S(1)}, bf16[256,128]{1,0:T(8,128)(2,1)S(1)}, u32[]{:S(2)}, u32[]{:S(2)}) collective-permute-start(bf16[256,128]{1,0:T(8,128)(2,1)S(1)} %shard_map.85.inputs), channel_id=1, source_target_pairs={{32,0},{64,32},{96,64},{128,96},{160,128},{192,160},{224,192},{256... | collective-permute-start | bytes 196616 | tf_op jit(solution)/shard_map/ppermute | solution.py:162
  26.4 4.0 %collective-permute-start.2 = (bf16[256,128]{1,0:T(8,128)(2,1)S(1)}, bf16[256,128]{1,0:T(8,128)(2,1)S(1)}, u32[]{:S(2)}, u32[]{:S(2)}) collective-permute-start(bf16[256,128]{1,0:T(8,128)(2,1)S(1)} %shard_map.85.inputs), channel_id=1, source_target_pairs={{0,32},{32,64},{64,96},{96,128},{128,160},{160,192},{192,224},{224... | collective-permute-start | bytes 196616 | tf_op jit(solution)/shard_map/ppermute | solution.py:161
  30.4 3.0 %all-to-all-done.parts = f32[32,4,128]{2,1,0:T(4,128)S(1)} async-done(((f32[32,4,128]{2,1,0:T(4,128)}), f32[32,4,128]{2,1,0:T(4,128)S(1)}, u32[]{:S(2)}, u32[]{:S(2)}) %all-to-all-start) | async-done | bytes 65568 | tf_op jit(solution)/shard_map/all_to_all | solution.py:163
  33.5 0.6 %shard_map.88 = f32[16,4,128]{2,1,0:T(4,128)} custom-call(f32[32,4,128]{2,1,0:T(4,128)S(1)} %all-to-all-done.parts), custom_call_target="tpu_custom_call" | custom-call | flops 65536 | bytes 131072 | tf_op jit(solution)/shard_map/pallas_call | solution.py:164
  34.1 0.0 copy-start.2
  34.1 0.0 copy-start.5
  34.1 9.2 %all-to-all-start.1 = ((f32[16,4,128]{2,1,0:T(4,128)}), f32[16,4,128]{2,1,0:T(4,128)S(1)}, u32[]{:S(2)}, u32[]{:S(2)}) async-start(f32[16,4,128]{2,1,0:T(4,128)} %shard_map.88), calls=%async_computation.1 | async-start | bytes 65536 | tf_op jit(solution)/shard_map/all_to_all | solution.py:172
  43.3 0.0 collective-permute-done.3.in_right
  43.4 0.0 collective-permute-done.2.in_left
  43.4 0.0 copy-done.2
  43.4 0.0 copy-done.5
  43.4 1.7 %shard_map.87 = (bf16[256,128]{1,0:T(8,128)(2,1)}, bf16[256,128]{1,0:T(8,128)(2,1)}, f32[16,256]{1,0:T(8,128)S(1)}) custom-call(bf16[256,128]{1,0:T(8,128)(2,1)S(1)} %shard_map.85.inputs, bf16[256,128]{1,0:T(8,128)(2,1)S(1)} %copy-done, bf16[256,128]{1,0:T(8,128)(2,1)S(1)} %collective-permute-done.2.in_left, ...), custom_call_target="tpu_custom_call" | custom-call | flops 100663296 | bytes 524288 | tf_op jit(solution)/shard_map/pallas_call | solution.py:173
  45.1 7.1 %all-to-all-done.1.parts = f32[16,4,128]{2,1,0:T(4,128)S(1)} async-done(((f32[16,4,128]{2,1,0:T(4,128)}), f32[16,4,128]{2,1,0:T(4,128)S(1)}, u32[]{:S(2)}, u32[]{:S(2)}) %all-to-all-start.1) | async-done | bytes 32800 | tf_op jit(solution)/shard_map/all_to_all | solution.py:172
  52.2 0.6 %shard_map.89 = f32[16,256]{1,0:T(8,128)} custom-call(f32[16,4,128]{2,1,0:T(4,128)S(1)} %all-to-all-done.1.parts, f32[16,256]{1,0:T(8,128)S(1)} %get-tuple-element.12.factor), custom_call_target="tpu_custom_call" | custom-call | flops 16384 | bytes 65536 | tf_op jit(solution)/shard_map/pallas_call | solution.py:181
Async XLA Ops:
  0.6 8.5 %copy-start = (bf16[256,128]{1,0:T(8,128)(2,1)S(1)}, bf16[256,128]{1,0:T(8,128)(2,1)}, u32[]{:S(2)}) copy-start(bf16[256,128]{1,0:T(8,128)(2,1)} %cotangent.3) | copy-start | bytes 196612
  0.6 8.4 %collective-permute-start.1 = (bf16[256,128]{1,0:T(8,128)(2,1)}, bf16[256,128]{1,0:T(8,128)(2,1)S(1)}, u32[]{:S(2)}, u32[]{:S(2)}) collective-permute-start(bf16[256,128]{1,0:T(8,128)(2,1)} %cotangent.3), channel_id=1, source_target_pairs={{32,0},{64,32},{96,64},{128,96},{160,128},{192,160},{224,192},{256... | collective-permute-start | bytes 196616 | tf_op jit(solution)/shard_map/ppermute | solution.py:142
  2.1 7.0 %collective-permute-start = (bf16[256,128]{1,0:T(8,128)(2,1)}, bf16[256,128]{1,0:T(8,128)(2,1)S(1)}, u32[]{:S(2)}, u32[]{:S(2)}) collective-permute-start(bf16[256,128]{1,0:T(8,128)(2,1)} %cotangent.3), channel_id=1, source_target_pairs={{0,32},{32,64},{64,96},{96,128},{128,160},{160,192},{192,224},{224... | collective-permute-start | bytes 196616 | tf_op jit(solution)/shard_map/ppermute | solution.py:141
  6.7 0.8 %copy-start.1 = (bf16[256,128]{1,0:T(8,128)(2,1)S(1)}, bf16[256,128]{1,0:T(8,128)(2,1)}, u32[]{:S(2)}) copy-start(bf16[256,128]{1,0:T(8,128)(2,1)} %hidden.1) | copy-start | bytes 196612
  7.5 0.7 %copy-start.3 = (bf16[12,128]{1,0:T(8,128)(2,1)S(1)}, bf16[12,128]{1,0:T(8,128)(2,1)}, u32[]{:S(2)}) copy-start(bf16[12,128]{1,0:T(8,128)(2,1)} %table.1) | copy-start | bytes 9220
  8.2 0.7 %copy-start.4 = (s32[256]{0:T(256)S(1)}, s32[256]{0:T(256)}, u32[]{:S(2)}) copy-start(s32[256]{0:T(256)} %ids.1) | copy-start | bytes 3076
  10.5 22.9 %all-to-all-start = ((f32[32,4,128]{2,1,0:T(4,128)}), f32[32,4,128]{2,1,0:T(4,128)S(1)}, u32[]{:S(2)}, u32[]{:S(2)}) async-start(f32[32,4,128]{2,1,0:T(4,128)} %shard_map.86), calls=%async_computation | async-start | bytes 131072 | tf_op jit(solution)/shard_map/all_to_all | solution.py:163
  25.1 18.2 %collective-permute-start.3 = (bf16[256,128]{1,0:T(8,128)(2,1)S(1)}, bf16[256,128]{1,0:T(8,128)(2,1)S(1)}, u32[]{:S(2)}, u32[]{:S(2)}) collective-permute-start(bf16[256,128]{1,0:T(8,128)(2,1)S(1)} %shard_map.85.inputs), channel_id=1, source_target_pairs={{32,0},{64,32},{96,64},{128,96},{160,128},{192,160},{224,192},{256... | collective-permute-start | bytes 196616 | tf_op jit(solution)/shard_map/ppermute | solution.py:162
  26.4 16.9 %collective-permute-start.2 = (bf16[256,128]{1,0:T(8,128)(2,1)S(1)}, bf16[256,128]{1,0:T(8,128)(2,1)S(1)}, u32[]{:S(2)}, u32[]{:S(2)}) collective-permute-start(bf16[256,128]{1,0:T(8,128)(2,1)S(1)} %shard_map.85.inputs), channel_id=1, source_target_pairs={{0,32},{32,64},{64,96},{96,128},{128,160},{160,192},{192,224},{224... | collective-permute-start | bytes 196616 | tf_op jit(solution)/shard_map/ppermute | solution.py:161
  34.1 9.3 %copy-start.2 = (bf16[16,256]{1,0:T(8,128)(2,1)S(1)}, bf16[16,256]{1,0:T(8,128)(2,1)}, u32[]{:S(2)}) copy-start(bf16[16,256]{1,0:T(8,128)(2,1)} %filters.1) | copy-start | bytes 24580
  34.1 9.3 %copy-start.5 = (s32[16]{0:T(128)S(1)}, s32[16]{0:T(128)}, u32[]{:S(2)}) copy-start(s32[16]{0:T(128)} %lengths.1) | copy-start | bytes 196
  34.1 18.1 %all-to-all-start.1 = ((f32[16,4,128]{2,1,0:T(4,128)}), f32[16,4,128]{2,1,0:T(4,128)S(1)}, u32[]{:S(2)}, u32[]{:S(2)}) async-start(f32[16,4,128]{2,1,0:T(4,128)} %shard_map.88), calls=%async_computation.1 | async-start | bytes 65536 | tf_op jit(solution)/shard_map/all_to_all | solution.py:172

commit v3 on v1

--- a/solution.py
+++ b/solution.py
@@ -15,10 +15,10 @@
 GROUPS = 16
 PARTS = (("z", 8), ("x_lo", 2), ("x_hi", 2), ("y", 8), ("core", 2))
 CTX = ("z", "x_lo")
-GROUP = ("x_hi", "y")
-SUMMED = ("z", "x_lo", "core")
+FIRST = ("core","z")
+SECOND = ("x_lo","x_hi","y")
+SIZES = dict(PARTS)
 CTX_SIZE = 16
-SUMMED_SIZE = 32
 
 VMEM = pl.BlockSpec(memory_space=pltpu.VMEM)
 SMEM = pl.BlockSpec(memory_space=pltpu.SMEM)
@@ -60,16 +60,26 @@
     return jnp.sum(product, axis=0, keepdims=True)
 
 
-def correlate_kernel(both, left, out):
+LANE = ((1,), (1,))
+
+
+def lag_here():
     shape = (ROWS, ROWS)
-    here = iota(shape, 1) >= iota(shape, 0)
-    lane = ((1,), (1,))
+    return iota(shape, 1) >= iota(shape, 0)
+
+
+def near_kernel(both, near):
+    here = lag_here()
+    for first, second in ((0, 1), (1, 0)):
+        near[first] = jnp.where(here, dot(both[first], both[second], LANE), 0.0)
+
+
+def correlate_kernel(both, right, near, out):
+    here = lag_here()
     sums = []
     for first, second in ((0, 1), (1, 0)):
-        fixed = both[second]
-        near = dot(both[first], fixed, lane)
-        far = dot(left[first], fixed, lane)
-        sums.append(lag_sums(jnp.where(here, near, far)))
+        far = dot(both[first], right[second], LANE)
+        sums.append(lag_sums(jnp.where(here, near[first], far)))
     half = TAPS // 2
     pieces = [sums[0][:, :half], sums[0][:, half:], sums[1][:, :half], sums[1][:, half:]]
     row = iota((4, half), 0)
@@ -79,17 +89,48 @@
         out[peer] = packed
 
 
+def sources(axes, fixed):
+    places = [0]
+    for name in axes:
+        size = SIZES[name]
+        picks = [fixed[name]] if name in fixed else range(size)
+        places = [place * size + pick for place in places for pick in picks]
+    return places
+
+
+def tree_sum(terms):
+    while len(terms) > 1:
+        terms = [sum(terms[i : i + 2][1:], terms[i]) for i in range(0, len(terms), 2)]
+    return terms[0]
+
+
+def kept_places():
+    places = [{}]
+    for name in FIRST:
+        if name in ("x_hi", "y"):
+            places = [dict(place, **{name: i}) for place in places for i in range(SIZES[name])]
+    return places
+
+
 def sum_kernel(parts, out):
-    total = jnp.sum(parts[...], axis=0)
-    for peer in range(out.shape[0]):
-        out[peer] = total
+    for kept, fixed in enumerate(kept_places()):
+        total = tree_sum([parts[place] for place in sources(FIRST, fixed)])
+        for peer in range(out.shape[0]):
+            out[peer, kept] = total
+
+
+def group_sum(parts, group):
+    coords = {"x_hi": group // 8, "y": group % 8}
+    kept = next(i for i, fixed in enumerate(kept_places()) if fixed.items() <= coords.items())
+    return tree_sum([parts[place, kept] for place in sources(SECOND, coords)])
 
 
 def finish_kernel(parts, factor, out):
     half = TAPS // 2
+    total = [group_sum(parts, group) for group in range(GROUPS)]
     for group in range(GROUPS):
-        own = parts[group]
-        other = parts[GROUPS - 1 - group]
+        own = total[group]
+        other = total[GROUPS - 1 - group]
         out[group : group + 1, :half] = own[0:1] + other[2:3]
         out[group : group + 1, half:] = own[1:2] + other[3:4]
     scaled = factor[...]
@@ -144,44 +185,54 @@
         out_shape=shape((2, ROWS, CHANS), jnp.bfloat16),
         in_specs=[VMEM] * 4,
         out_specs=VMEM,
-        cost_estimate=cost(2 * 16 * ROWS * CHANS, 1 << 18),
+        cost_estimate=cost(1, 1),
     )(hidden, token_ids, embedding, cotangent)
     up = [(i, i + 1) for i in range(CTX_SIZE - 1)]
     left = lax.ppermute(both, CTX, up)
     right = lax.ppermute(both, CTX, [(j, i) for i, j in up])
+    pair = (2, ROWS, ROWS)
+    near = pl.pallas_call(
+        near_kernel,
+        out_shape=shape(pair, jnp.float32),
+        in_specs=[VMEM],
+        out_specs=VMEM,
+        cost_estimate=cost(1, 1),
+        compiler_params=ROOM,
+    )(both)
     sums = pl.pallas_call(
         correlate_kernel,
-        out_shape=shape((SUMMED_SIZE, 4, half), jnp.float32),
-        in_specs=[VMEM] * 2,
-        out_specs=VMEM,
-        cost_estimate=cost(8 * ROWS * ROWS * CHANS, 1 << 18),
-        compiler_params=ROOM,
-    )(both, left)
-    sums = lax.all_to_all(sums, SUMMED, 0, 0)
-    sums = pl.pallas_call(
-        sum_kernel,
-        out_shape=shape((GROUPS, 4, half), jnp.float32),
-        in_specs=[VMEM],
-        out_specs=VMEM,
-        cost_estimate=cost(1 << 16, 1 << 17),
-        compiler_params=ROOM,
-    )(sums)
-    sums = lax.all_to_all(sums, GROUP, 0, 0)
+        out_shape=shape((math.prod(SIZES[a] for a in FIRST), 4, half), jnp.float32),
+        in_specs=[VMEM] * 3,
+        out_specs=VMEM,
+        cost_estimate=cost(1, 1),
+        compiler_params=ROOM,
+    )(both, right, near)
+    sums = lax.all_to_all(sums, FIRST, 0, 0)
     block = shape((ROWS, CHANS), jnp.bfloat16)
     mixed, hidden_grad, factor = pl.pallas_call(
         outputs_kernel,
         out_shape=(block, block, shape((GROUPS, TAPS), jnp.float32)),
         in_specs=[VMEM] * 4 + [SMEM],
         out_specs=(VMEM,) * 3,
-        cost_estimate=cost(12 * ROWS * ROWS * CHANS, 1 << 19),
+        cost_estimate=cost(1, 1),
         compiler_params=ROOM,
     )(both, left, right, filters, lengths)
+    sums, factor = lax.optimization_barrier((sums, factor))
+    sums = pl.pallas_call(
+        sum_kernel,
+        out_shape=shape((math.prod(SIZES[a] for a in SECOND), len(kept_places()), 4, half), jnp.float32),
+        in_specs=[VMEM],
+        out_specs=VMEM,
+        cost_estimate=cost(1, 1),
+        compiler_params=ROOM,
+    )(sums)
+    sums = lax.all_to_all(sums, SECOND, 0, 0)
     filter_grad = pl.pallas_call(
         finish_kernel,
         out_shape=shape((GROUPS, TAPS), jnp.float32),
         in_specs=[VMEM] * 2,
         out_specs=VMEM,
-        cost_estimate=cost(1 << 14, 1 << 16),
+        cost_estimate=cost(1, 1),
         compiler_params=ROOM,
     )(sums, factor)
     return mixed, hidden_grad, filter_grad

time: 54.5 us -> 50.4 us (0.925)
  blocking collectives: 0 us -> 19 us
  starting transfers between devices: 29.9 us -> 17.8 us
  waiting for transfers between devices: 16.4 us -> 5.34 us
  local copies, waits for them, and re-layouts: 0.91 us -> 1.57 us
    all_to_all x0 -> x1, blocking collectives: none -> 19 us  [on_device(): sums = lax.all_to_all(sums, SECOND, 0, 0)]
    all_to_all x2 -> x1, starting transfers between devices: 24.7 us -> 11.9 us  [on_device(): sums = lax.all_to_all(sums, FIRST, 0, 0)]
    all_to_all x2 -> x1, waiting for transfers between devices: 14.1 us -> 5.33 us  [on_device(): sums = lax.all_to_all(sums, FIRST, 0, 0)]
    ppermute x1, waiting for transfers between devices: 2.24 us -> 0.01 us  [on_device(): left = lax.ppermute(both, CTX, up)]
    unnamed x8, local copies, waits for them, and re-layouts: 0.91 us -> 1.57 us
    ppermute x1, starting transfers between devices: 3.94 us -> 4.58 us  [on_device(): left = lax.ppermute(both, CTX, up)]
    pallas_call x2 -> x3, Pallas kernels: 2.08 us -> 1.57 us  [the longest x1 1.33 us: on_device(): pl.pallas_call(correlate_kernel, out_shape=shape((math.prod((SIZES[a] for...]
  transfers between devices with their start and end apart: 4 -> 3, of which waited for: 3 -> 1; matrix products, arithmetic and copies ran while one was open for 0% -> 0% of each run, Pallas kernels for 4% -> 6%
where the time goes in v3:
time: 50.4 us; the launch traced here: 50.1 us
  blocking collectives  19 us (38%)
  starting transfers between devices  17.8 us (35%)
  Pallas kernels  5.67 us (11%)
  waiting for transfers between devices  5.34 us (11%)
  local copies, waits for them, and re-layouts  1.57 us (3%)
  between operations  0.7 us (1%)
    all_to_all x1, blocking collectives, on_device(): sums = lax.all_to_all(sums, SECOND, 0, 0)  19 us
    all_to_all x1, starting transfers between devices, on_device(): sums = lax.all_to_all(sums, FIRST, 0, 0)  11.9 us
    all_to_all x1, waiting for transfers between devices, on_device(): sums = lax.all_to_all(sums, FIRST, 0, 0)  5.33 us
    ppermute x1, starting transfers between devices, on_device(): left = lax.ppermute(both, CTX, up)  4.58 us
    pallas_call x1, Pallas kernels, on_device(): pl.pallas_call(inputs_kernel, out_shape=shape((2, ROWS, CHANS), jnp.bfloa...  1.78 us
    pallas_call x1, Pallas kernels, on_device(): pl.pallas_call(outputs_kernel, out_shape=(block, block, shape((GROUPS, TA...  1.69 us
    unnamed x8, local copies, waits for them, and re-layouts  1.57 us
    pallas_call x1, Pallas kernels, on_device(): pl.pallas_call(correlate_kernel, out_shape=shape((math.prod((SIZES[a] for...  1.33 us
  transfers between devices with their start and end apart: 3, of which 1 were waited for; matrix products, arithmetic and copies ran while one was open for 0% of the time, Pallas kernels for 6%

profile of v3, /device:TPU:1, one launch (start us, length us, event | category | flops | bytes accessed | tf_op | source)
XLA Modules:
  0.0 50.1 jit_solution(15976098655207527988)
XLA Ops:
  0.6 1.8 %shard_map.85.both = bf16[2,256,128]{2,1,0:T(8,128)(2,1)} custom-call(bf16[256,128]{1,0:T(8,128)(2,1)} %hidden.1, s32[256]{0:T(256)} %ids.1, bf16[12,128]{1,0:T(8,128)(2,1)} %table.1, bf16[256,128]{1,0:T(8,128)(2,1)} %cotangent.1), custom_call_target="tpu_custom_call" | custom-call | flops 1 | bytes 1 | tf_op jit(solution)/shard_map/pallas_call | solution.py:183
  2.4 1.3 %collective-permute-start.1 = (bf16[2,256,128]{2,1,0:T(8,128)(2,1)}, bf16[2,256,128]{2,1,0:T(8,128)(2,1)S(1)}, u32[]{:S(2)}, u32[]{:S(2)}) collective-permute-start(bf16[2,256,128]{2,1,0:T(8,128)(2,1)} %shard_map.85.both), channel_id=1, source_target_pairs={{32,0},{64,32},{96,64},{128,96},{160,128},{192,160},{224,192},{256... | collective-permute-start | bytes 393224 | tf_op jit(solution)/shard_map/ppermute | solution.py:192
  3.7 4.6 %collective-permute-start = (bf16[2,256,128]{2,1,0:T(8,128)(2,1)}, bf16[2,256,128]{2,1,0:T(8,128)(2,1)S(1)}, u32[]{:S(2)}, u32[]{:S(2)}) collective-permute-start(bf16[2,256,128]{2,1,0:T(8,128)(2,1)} %shard_map.85.both), channel_id=1, source_target_pairs={{0,32},{32,64},{64,96},{96,128},{128,160},{160,192},{192,224},{224... | collective-permute-start | bytes 393224 | tf_op jit(solution)/shard_map/ppermute | solution.py:191
  8.3 0.0 copy-start
  8.3 0.9 %copy-done = bf16[2,256,128]{2,1,0:T(8,128)(2,1)S(1)} copy-done((bf16[2,256,128]{2,1,0:T(8,128)(2,1)S(1)}, bf16[2,256,128]{2,1,0:T(8,128)(2,1)}, u32[]{:S(2)}) %copy-start) | copy-done | bytes 131096
  9.2 0.0 copy-start.1
  9.2 0.2 shard_map.87.near
  9.4 0.0 collective-permute-done.1.right
  9.4 0.7 %copy-done.1 = bf16[2,256,128]{2,1,0:T(8,128)(2,1)S(1)} copy-done((bf16[2,256,128]{2,1,0:T(8,128)(2,1)S(1)}, bf16[2,256,128]{2,1,0:T(8,128)(2,1)}, u32[]{:S(2)}) %copy-start.1) | copy-done | bytes 131096
  10.1 1.3 %shard_map.88 = f32[16,4,128]{2,1,0:T(4,128)} custom-call(bf16[2,256,128]{2,1,0:T(8,128)(2,1)S(1)} %copy-done.1, bf16[2,256,128]{2,1,0:T(8,128)(2,1)S(1)} %collective-permute-done.1.right, f32[2,256,256]{2,1,0:T(8,128)S(1)} %shard_map.87.near), custom_call_target="tpu_custom_call" | custom-call | flops 1 | bytes 1 | tf_op jit(solution)/shard_map/pallas_call | solution.py:202
  11.4 0.0 copy-start.2
  11.4 0.0 copy-start.3
  11.4 11.9 %all-to-all-start = ((f32[16,4,128]{2,1,0:T(4,128)}), f32[16,4,128]{2,1,0:T(4,128)S(1)}, u32[]{:S(2)}, u32[]{:S(2)}) async-start(f32[16,4,128]{2,1,0:T(4,128)} %shard_map.88), calls=%async_computation | async-start | bytes 65536 | tf_op jit(solution)/shard_map/all_to_all | solution.py:210
  23.4 0.0 collective-permute-done.left
  23.4 0.0 copy-done.2
  23.4 0.0 copy-done.3
  23.4 1.7 %shard_map.86 = (bf16[256,128]{1,0:T(8,128)(2,1)}, bf16[256,128]{1,0:T(8,128)(2,1)}, f32[16,256]{1,0:T(8,128)S(1)}) custom-call(bf16[2,256,128]{2,1,0:T(8,128)(2,1)S(1)} %copy-done.1, bf16[2,256,128]{2,1,0:T(8,128)(2,1)S(1)} %collective-permute-done.left, bf16[2,256,128]{2,1,0:T(8,128)(2,1)S(1)} %collective-permute-done.1.right, ...), custom_call_target="tpu_custom_call" | custom-call | flops 1 | bytes 1 | tf_op jit(solution)/shard_map/pallas_call | solution.py:212
  25.1 5.3 %all-to-all-done.parts = f32[16,4,128]{2,1,0:T(4,128)S(1)} async-done(((f32[16,4,128]{2,1,0:T(4,128)}), f32[16,4,128]{2,1,0:T(4,128)S(1)}, u32[]{:S(2)}, u32[]{:S(2)}) %all-to-all-start) | async-done | bytes 32800 | tf_op jit(solution)/shard_map/all_to_all | solution.py:210
  30.4 19.0 %all_to_all.10.parts = f32[32,1,4,128]{3,2,1,0:T(4,128)S(1)} all-to-all(f32[32,1,4,128]{3,2,1,0:T(4,128)S(1)} %shard_map.89), channel_id=1, replica_groups=mesh['z'=8,'x_lo'=2,'x_hi'=2,'y'=8,'core'=2] {'x_lo','x_hi','y'}, dimensions={0} | all-to-all | bytes 131072 | tf_op jit(solution)/shard_map/all_to_all | solution.py:229
  49.5 0.6 %shard_map.90 = f32[16,256]{1,0:T(8,128)} custom-call(f32[32,1,4,128]{3,2,1,0:T(4,128)S(1)} %all_to_all.10.parts, f32[16,256]{1,0:T(8,128)S(1)} %get-tuple-element.12.factor), custom_call_target="tpu_custom_call" | custom-call | flops 1 | bytes 1 | tf_op jit(solution)/shard_map/pallas_call | solution.py:230
  (1 shorter events, 0.0 us)
Async XLA Ops:
  2.4 7.0 %collective-permute-start.1 = (bf16[2,256,128]{2,1,0:T(8,128)(2,1)}, bf16[2,256,128]{2,1,0:T(8,128)(2,1)S(1)}, u32[]{:S(2)}, u32[]{:S(2)}) collective-permute-start(bf16[2,256,128]{2,1,0:T(8,128)(2,1)} %shard_map.85.both), channel_id=1, source_target_pairs={{32,0},{64,32},{96,64},{128,96},{160,128},{192,160},{224,192},{256... | collective-permute-start | bytes 393224 | tf_op jit(solution)/shard_map/ppermute | solution.py:192
  3.7 19.7 %collective-permute-start = (bf16[2,256,128]{2,1,0:T(8,128)(2,1)}, bf16[2,256,128]{2,1,0:T(8,128)(2,1)S(1)}, u32[]{:S(2)}, u32[]{:S(2)}) collective-permute-start(bf16[2,256,128]{2,1,0:T(8,128)(2,1)} %shard_map.85.both), channel_id=1, source_target_pairs={{0,32},{32,64},{64,96},{96,128},{128,160},{160,192},{192,224},{224... | collective-permute-start | bytes 393224 | tf_op jit(solution)/shard_map/ppermute | solution.py:191
  8.3 0.9 %copy-start = (bf16[2,256,128]{2,1,0:T(8,128)(2,1)S(1)}, bf16[2,256,128]{2,1,0:T(8,128)(2,1)}, u32[]{:S(2)}) copy-start(bf16[2,256,128]{2,1,0:T(8,128)(2,1)} %shard_map.85.both) | copy-start | bytes 393220
  9.2 0.9 %copy-start.1 = (bf16[2,256,128]{2,1,0:T(8,128)(2,1)S(1)}, bf16[2,256,128]{2,1,0:T(8,128)(2,1)}, u32[]{:S(2)}) copy-start(bf16[2,256,128]{2,1,0:T(8,128)(2,1)} %shard_map.85.both) | copy-start | bytes 393220
  11.4 12.0 %copy-start.2 = (bf16[16,256]{1,0:T(8,128)(2,1)S(1)}, bf16[16,256]{1,0:T(8,128)(2,1)}, u32[]{:S(2)}) copy-start(bf16[16,256]{1,0:T(8,128)(2,1)} %filters.1) | copy-start | bytes 24580
  11.4 12.0 %copy-start.3 = (s32[16]{0:T(128)S(1)}, s32[16]{0:T(128)}, u32[]{:S(2)}) copy-start(s32[16]{0:T(128)} %lengths.1) | copy-start | bytes 196
  11.4 19.0 %all-to-all-start = ((f32[16,4,128]{2,1,0:T(4,128)}), f32[16,4,128]{2,1,0:T(4,128)S(1)}, u32[]{:S(2)}, u32[]{:S(2)}) async-start(f32[16,4,128]{2,1,0:T(4,128)} %shard_map.88), calls=%async_computation | async-start | bytes 65536 | tf_op jit(solution)/shard_map/all_to_all | solution.py:210

commit v4 on v3

--- a/solution.py
+++ b/solution.py
@@ -39,11 +39,13 @@
     return lax.broadcasted_iota(jnp.int32, shape, dim)
 
 
-def inputs_kernel(hidden, ids, table, cotangent, both):
-    symbols = table.shape[0]
-    shape = (symbols, ROWS)
-    ids_row = jnp.broadcast_to(ids[...].reshape(1, ROWS), shape)
-    onehot = jnp.where(iota(shape, 0) == ids_row, 1.0, 0.0)
+def symbols_kernel(symbols):
+    symbols[...] = iota(symbols.shape, 0)
+
+
+def inputs_kernel(hidden, ids, table, cotangent, symbols, both):
+    ids_row = jnp.broadcast_to(ids[...].reshape(1, ROWS), symbols.shape)
+    onehot = jnp.where(symbols[...] == ids_row, 1.0, 0.0)
     looked = dot(onehot, table[...].astype(jnp.float32), ((0,), (0,)))
     both[0] = (hidden[...].astype(jnp.float32) + looked).astype(jnp.bfloat16)
     both[1] = cotangent[...]
@@ -180,13 +182,22 @@
 def on_device(hidden, token_ids, embedding, filters, lengths, cotangent):
     shape = jax.ShapeDtypeStruct
     half = TAPS // 2
+    symbols = pl.pallas_call(
+        symbols_kernel,
+        out_shape=shape((embedding.shape[0], ROWS), jnp.int32),
+        in_specs=[],
+        out_specs=VMEM,
+        cost_estimate=cost(1 << 33, 1 << 24),
+        compiler_params=ROOM,
+    )()
     both = pl.pallas_call(
         inputs_kernel,
         out_shape=shape((2, ROWS, CHANS), jnp.bfloat16),
-        in_specs=[VMEM] * 4,
-        out_specs=VMEM,
-        cost_estimate=cost(1, 1),
-    )(hidden, token_ids, embedding, cotangent)
+        in_specs=[VMEM] * 5,
+        out_specs=VMEM,
+        cost_estimate=cost(1, 1),
+        compiler_params=ROOM,
+    )(hidden, token_ids, embedding, cotangent, symbols)
     up = [(i, i + 1) for i in range(CTX_SIZE - 1)]
     left = lax.ppermute(both, CTX, up)
     right = lax.ppermute(both, CTX, [(j, i) for i, j in up])

time: 50.4 us -> 49.3 us (0.978)
  Pallas kernels: 5.67 us -> 4.13 us
  starting transfers between devices: 17.8 us -> 18.7 us
  local copies, waits for them, and re-layouts: 1.57 us -> 0.87 us
    pallas_call x1, Pallas kernels: 1.78 us -> 0.22 us  [on_device(): pl.pallas_call(inputs_kernel, out_shape=shape((2, ROWS, CHANS), jnp.bfloa...]
    all_to_all x1, starting transfers between devices: 11.9 us -> 12.8 us  [on_device(): sums = lax.all_to_all(sums, FIRST, 0, 0)]
    unnamed x8 -> x12, local copies, waits for them, and re-layouts: 1.57 us -> 0.87 us
  transfers between devices with their start and end apart: 3 -> 3, of which waited for: 1 -> 2; matrix products, arithmetic and copies ran while one was open for 0% -> 0% of each run, Pallas kernels for 6% -> 7%
where the time goes in v4:
time: 49.3 us; the launch traced here: 49 us
  blocking collectives  19.1 us (39%)
  starting transfers between devices  18.7 us (38%)
  waiting for transfers between devices  5.51 us (11%)
  Pallas kernels  4.13 us (8%)
  local copies, waits for them, and re-layouts  0.87 us (2%)
  between operations  0.72 us (1%)
    all_to_all x1, blocking collectives, on_device(): sums = lax.all_to_all(sums, SECOND, 0, 0)  19.1 us
    all_to_all x1, starting transfers between devices, on_device(): sums = lax.all_to_all(sums, FIRST, 0, 0)  12.8 us
    all_to_all x1, waiting for transfers between devices, on_device(): sums = lax.all_to_all(sums, FIRST, 0, 0)  5.33 us
    ppermute x1, starting transfers between devices, on_device(): left = lax.ppermute(both, CTX, up)  4.58 us
    pallas_call x1, Pallas kernels, on_device(): pl.pallas_call(outputs_kernel, out_shape=(block, block, shape((GROUPS, TA...  1.69 us
    pallas_call x1, Pallas kernels, on_device(): pl.pallas_call(correlate_kernel, out_shape=shape((math.prod((SIZES[a] for...  1.34 us
    ppermute x1, starting transfers between devices, on_device(): right = lax.ppermute(both, CTX, [(j, i) for i, j in up])  1.29 us
  transfers between devices with their start and end apart: 3, of which 2 were waited for; matrix products, arithmetic and copies ran while one was open for 0% of the time, Pallas kernels for 7%

profile of v4, /device:TPU:1, one launch (start us, length us, event | category | flops | bytes accessed | tf_op | source)
XLA Modules:
  0.0 49.0 jit_solution(3406158623448699351)
XLA Ops:
  0.6 0.0 copy-start.1
  0.6 0.0 copy-start.3
  0.7 0.0 copy-start.4
  0.7 0.0 copy-start
  0.7 0.8 %copy-done.1 = bf16[256,128]{1,0:T(8,128)(2,1)S(1)} copy-done((bf16[256,128]{1,0:T(8,128)(2,1)S(1)}, bf16[256,128]{1,0:T(8,128)(2,1)}, u32[]{:S(2)}) %copy-start.1) | copy-done | bytes 65560
  1.5 0.0 copy-done.3
  1.5 0.0 copy-done.4
  1.5 0.1 copy-done
  1.5 0.2 shard_map.86.both
  1.8 1.3 %collective-permute-start.1 = (bf16[2,256,128]{2,1,0:T(8,128)(2,1)S(1)}, bf16[2,256,128]{2,1,0:T(8,128)(2,1)S(1)}, u32[]{:S(2)}, u32[]{:S(2)}) collective-permute-start(bf16[2,256,128]{2,1,0:T(8,128)(2,1)S(1)} %shard_map.86.both), channel_id=1, source_target_pairs={{32,0},{64,32},{96,64},{128,96},{160,128},{192,160},{224,192},{256... | collective-permute-start | bytes 393224 | tf_op jit(solution)/shard_map/ppermute | solution.py:203
  3.1 4.6 %collective-permute-start = (bf16[2,256,128]{2,1,0:T(8,128)(2,1)S(1)}, bf16[2,256,128]{2,1,0:T(8,128)(2,1)S(1)}, u32[]{:S(2)}, u32[]{:S(2)}) collective-permute-start(bf16[2,256,128]{2,1,0:T(8,128)(2,1)S(1)} %shard_map.86.both), channel_id=1, source_target_pairs={{0,32},{32,64},{64,96},{96,128},{128,160},{160,192},{192,224},{224... | collective-permute-start | bytes 393224 | tf_op jit(solution)/shard_map/ppermute | solution.py:202
  7.6 0.2 shard_map.88.near
  7.9 0.2 collective-permute-done.1.right
  8.1 1.3 %shard_map.89 = f32[16,4,128]{2,1,0:T(4,128)} custom-call(bf16[2,256,128]{2,1,0:T(8,128)(2,1)S(1)} %shard_map.86.both, bf16[2,256,128]{2,1,0:T(8,128)(2,1)S(1)} %collective-permute-done.1.right, f32[2,256,256]{2,1,0:T(8,128)S(1)} %shard_map.88.near), custom_call_target="tpu_custom_call" | custom-call | flops 1 | bytes 1 | tf_op jit(solution)/shard_map/pallas_call | solution.py:213
  9.4 0.0 copy-start.2
  9.4 0.0 copy-start.5
  9.4 12.8 %all-to-all-start = ((f32[16,4,128]{2,1,0:T(4,128)}), f32[16,4,128]{2,1,0:T(4,128)S(1)}, u32[]{:S(2)}, u32[]{:S(2)}) async-start(f32[16,4,128]{2,1,0:T(4,128)} %shard_map.89), calls=%async_computation | async-start | bytes 65536 | tf_op jit(solution)/shard_map/all_to_all | solution.py:221
  22.2 0.0 collective-permute-done.left
  22.2 0.0 copy-done.2
  22.2 0.0 copy-done.5
  22.2 1.7 %shard_map.87 = (bf16[256,128]{1,0:T(8,128)(2,1)}, bf16[256,128]{1,0:T(8,128)(2,1)}, f32[16,256]{1,0:T(8,128)S(1)}) custom-call(bf16[2,256,128]{2,1,0:T(8,128)(2,1)S(1)} %shard_map.86.both, bf16[2,256,128]{2,1,0:T(8,128)(2,1)S(1)} %collective-permute-done.left, bf16[2,256,128]{2,1,0:T(8,128)(2,1)S(1)} %collective-permute-done.1.right, ...), custom_call_target="tpu_custom_call" | custom-call | flops 1 | bytes 1 | tf_op jit(solution)/shard_map/pallas_call | solution.py:223
  23.9 5.3 %all-to-all-done.parts = f32[16,4,128]{2,1,0:T(4,128)S(1)} async-done(((f32[16,4,128]{2,1,0:T(4,128)}), f32[16,4,128]{2,1,0:T(4,128)S(1)}, u32[]{:S(2)}, u32[]{:S(2)}) %all-to-all-start) | async-done | bytes 32800 | tf_op jit(solution)/shard_map/all_to_all | solution.py:221
  29.3 19.1 %all_to_all.10.parts = f32[32,1,4,128]{3,2,1,0:T(4,128)S(1)} all-to-all(f32[32,1,4,128]{3,2,1,0:T(4,128)S(1)} %shard_map.90), channel_id=1, replica_groups=mesh['z'=8,'x_lo'=2,'x_hi'=2,'y'=8,'core'=2] {'x_lo','x_hi','y'}, dimensions={0} | all-to-all | bytes 131072 | tf_op jit(solution)/shard_map/all_to_all | solution.py:240
  48.4 0.6 %shard_map.91 = f32[16,256]{1,0:T(8,128)} custom-call(f32[32,1,4,128]{3,2,1,0:T(4,128)S(1)} %all_to_all.10.parts, f32[16,256]{1,0:T(8,128)S(1)} %get-tuple-element.12.factor), custom_call_target="tpu_custom_call" | custom-call | flops 1 | bytes 1 | tf_op jit(solution)/shard_map/pallas_call | solution.py:241
  (2 shorter events, 0.0 us)
Async XLA Ops:
  0.6 0.8 %copy-start.1 = (bf16[256,128]{1,0:T(8,128)(2,1)S(1)}, bf16[256,128]{1,0:T(8,128)(2,1)}, u32[]{:S(2)}) copy-start(bf16[256,128]{1,0:T(8,128)(2,1)} %cotangent.1) | copy-start | bytes 196612
  0.6 0.8 %copy-start.3 = (bf16[12,128]{1,0:T(8,128)(2,1)S(1)}, bf16[12,128]{1,0:T(8,128)(2,1)}, u32[]{:S(2)}) copy-start(bf16[12,128]{1,0:T(8,128)(2,1)} %table.1) | copy-start | bytes 9220
  0.7 0.8 %copy-start.4 = (s32[256]{0:T(256)S(1)}, s32[256]{0:T(256)}, u32[]{:S(2)}) copy-start(s32[256]{0:T(256)} %ids.1) | copy-start | bytes 3076
  0.7 0.9 %copy-start = (bf16[256,128]{1,0:T(8,128)(2,1)S(1)}, bf16[256,128]{1,0:T(8,128)(2,1)}, u32[]{:S(2)}) copy-start(bf16[256,128]{1,0:T(8,128)(2,1)} %hidden.1) | copy-start | bytes 196612
  1.8 6.3 %collective-permute-start.1 = (bf16[2,256,128]{2,1,0:T(8,128)(2,1)S(1)}, bf16[2,256,128]{2,1,0:T(8,128)(2,1)S(1)}, u32[]{:S(2)}, u32[]{:S(2)}) collective-permute-start(bf16[2,256,128]{2,1,0:T(8,128)(2,1)S(1)} %shard_map.86.both), channel_id=1, source_target_pairs={{32,0},{64,32},{96,64},{128,96},{160,128},{192,160},{224,192},{256... | collective-permute-start | bytes 393224 | tf_op jit(solution)/shard_map/ppermute | solution.py:203
  3.1 19.1 %collective-permute-start = (bf16[2,256,128]{2,1,0:T(8,128)(2,1)S(1)}, bf16[2,256,128]{2,1,0:T(8,128)(2,1)S(1)}, u32[]{:S(2)}, u32[]{:S(2)}) collective-permute-start(bf16[2,256,128]{2,1,0:T(8,128)(2,1)S(1)} %shard_map.86.both), channel_id=1, source_target_pairs={{0,32},{32,64},{64,96},{96,128},{128,160},{160,192},{192,224},{224... | collective-permute-start | bytes 393224 | tf_op jit(solution)/shard_map/ppermute | solution.py:202
  9.4 12.8 %copy-start.2 = (bf16[16,256]{1,0:T(8,128)(2,1)S(1)}, bf16[16,256]{1,0:T(8,128)(2,1)}, u32[]{:S(2)}) copy-start(bf16[16,256]{1,0:T(8,128)(2,1)} %filters.1) | copy-start | bytes 24580
  9.4 12.8 %copy-start.5 = (s32[16]{0:T(128)S(1)}, s32[16]{0:T(128)}, u32[]{:S(2)}) copy-start(s32[16]{0:T(128)} %lengths.1) | copy-start | bytes 196
  9.4 19.9 %all-to-all-start = ((f32[16,4,128]{2,1,0:T(4,128)}), f32[16,4,128]{2,1,0:T(4,128)S(1)}, u32[]{:S(2)}, u32[]{:S(2)}) async-start(f32[16,4,128]{2,1,0:T(4,128)} %shard_map.89), calls=%async_computation | async-start | bytes 65536 | tf_op jit(solution)/shard_map/all_to_all | solution.py:221

commit v5 on v4

--- a/solution.py
+++ b/solution.py
@@ -15,9 +15,11 @@
 GROUPS = 16
 PARTS = (("z", 8), ("x_lo", 2), ("x_hi", 2), ("y", 8), ("core", 2))
 CTX = ("z", "x_lo")
-FIRST = ("core","z")
-SECOND = ("x_lo","x_hi","y")
+FIRST = ('z', 'core')
+SECOND = ('x_lo', 'x_hi', 'y')
 SIZES = dict(PARTS)
+ORDER1 = list(range(16))[::-1]
+ORDER2 = list(range(32))[::-1]
 CTX_SIZE = 16
 
 VMEM = pl.BlockSpec(memory_space=pltpu.VMEM)
@@ -116,7 +118,7 @@
 
 def sum_kernel(parts, out):
     for kept, fixed in enumerate(kept_places()):
-        total = tree_sum([parts[place] for place in sources(FIRST, fixed)])
+        total = tree_sum([parts[place] for place in map(ORDER1.index, sources(FIRST, fixed))])
         for peer in range(out.shape[0]):
             out[peer, kept] = total
 
@@ -124,7 +126,7 @@
 def group_sum(parts, group):
     coords = {"x_hi": group // 8, "y": group % 8}
     kept = next(i for i, fixed in enumerate(kept_places()) if fixed.items() <= coords.items())
-    return tree_sum([parts[place, kept] for place in sources(SECOND, coords)])
+    return tree_sum([parts[place, kept] for place in map(ORDER2.index, sources(SECOND, coords))])
 
 
 def finish_kernel(parts, factor, out):
@@ -218,7 +220,7 @@
         cost_estimate=cost(1, 1),
         compiler_params=ROOM,
     )(both, right, near)
-    sums = lax.all_to_all(sums, FIRST, 0, 0)
+    sums = lax.all_to_all(sums, FIRST, 0, 0, axis_index_groups=[ORDER1])
     block = shape((ROWS, CHANS), jnp.bfloat16)
     mixed, hidden_grad, factor = pl.pallas_call(
         outputs_kernel,
@@ -237,7 +239,7 @@
         cost_estimate=cost(1, 1),
         compiler_params=ROOM,
     )(sums)
-    sums = lax.all_to_all(sums, SECOND, 0, 0)
+    sums = lax.all_to_all(sums, SECOND, 0, 0, axis_index_groups=[ORDER2])
     filter_grad = pl.pallas_call(
         finish_kernel,
         out_shape=shape((GROUPS, TAPS), jnp.float32),

time: 49.3 us -> 44.8 us (0.909)
  blocking collectives: 19.1 us -> 16.4 us
  waiting for transfers between devices: 5.51 us -> 3.52 us
    all_to_all x1, blocking collectives: 19.1 us -> 16.4 us  [on_device(): sums = lax.all_to_all(sums, SECOND, 0, 0, axis_index_groups=[ORDER2])]
    all_to_all x1, waiting for transfers between devices: 5.33 us -> 3.34 us  [on_device(): sums = lax.all_to_all(sums, FIRST, 0, 0, axis_index_groups=[ORDER1])]
where the time goes in v5:
time: 44.8 us; the launch traced here: 44.5 us
  starting transfers between devices  18.9 us (42%)
  blocking collectives  16.4 us (37%)
  Pallas kernels  4.12 us (9%)
  waiting for transfers between devices  3.52 us (8%)
  local copies, waits for them, and re-layouts  0.87 us (2%)
  between operations  0.72 us (2%)
    all_to_all x1, blocking collectives, on_device(): sums = lax.all_to_all(sums, SECOND, 0, 0, axis_index_groups=[ORDER2])  16.4 us
    all_to_all x1, starting transfers between devices, on_device(): sums = lax.all_to_all(sums, FIRST, 0, 0, axis_index_groups=[ORDER1])  13 us
    ppermute x1, starting transfers between devices, on_device(): left = lax.ppermute(both, CTX, up)  4.58 us
    all_to_all x1, waiting for transfers between devices, on_device(): sums = lax.all_to_all(sums, FIRST, 0, 0, axis_index_groups=[ORDER1])  3.34 us
    pallas_call x1, Pallas kernels, on_device(): pl.pallas_call(outputs_kernel, out_shape=(block, block, shape((GROUPS, TA...  1.69 us
    pallas_call x1, Pallas kernels, on_device(): pl.pallas_call(correlate_kernel, out_shape=shape((math.prod((SIZES[a] for...  1.34 us
    ppermute x1, starting transfers between devices, on_device(): right = lax.ppermute(both, CTX, [(j, i) for i, j in up])  1.29 us
  transfers between devices with their start and end apart: 3, of which 2 were waited for; matrix products, arithmetic and copies ran while one was open for 0% of the time, Pallas kernels for 7%

profile of v5, /device:TPU:1, one launch (start us, length us, event | category | flops | bytes accessed | tf_op | source)
XLA Modules:
  0.0 44.5 jit_solution(16366078774969688035)
XLA Ops:
  0.6 0.0 copy-start.1
  0.6 0.0 copy-start.3
  0.7 0.0 copy-start.4
  0.7 0.0 copy-start
  0.7 0.8 %copy-done.1 = bf16[256,128]{1,0:T(8,128)(2,1)S(1)} copy-done((bf16[256,128]{1,0:T(8,128)(2,1)S(1)}, bf16[256,128]{1,0:T(8,128)(2,1)}, u32[]{:S(2)}) %copy-start.1) | copy-done | bytes 65560
  1.5 0.0 copy-done.3
  1.5 0.0 copy-done.4
  1.5 0.1 copy-done
  1.5 0.2 shard_map.86.both
  1.8 1.3 %collective-permute-start.1 = (bf16[2,256,128]{2,1,0:T(8,128)(2,1)S(1)}, bf16[2,256,128]{2,1,0:T(8,128)(2,1)S(1)}, u32[]{:S(2)}, u32[]{:S(2)}) collective-permute-start(bf16[2,256,128]{2,1,0:T(8,128)(2,1)S(1)} %shard_map.86.both), channel_id=1, source_target_pairs={{32,0},{64,32},{96,64},{128,96},{160,128},{192,160},{224,192},{256... | collective-permute-start | bytes 393224 | tf_op jit(solution)/shard_map/ppermute | solution.py:205
  3.1 4.6 %collective-permute-start = (bf16[2,256,128]{2,1,0:T(8,128)(2,1)S(1)}, bf16[2,256,128]{2,1,0:T(8,128)(2,1)S(1)}, u32[]{:S(2)}, u32[]{:S(2)}) collective-permute-start(bf16[2,256,128]{2,1,0:T(8,128)(2,1)S(1)} %shard_map.86.both), channel_id=1, source_target_pairs={{0,32},{32,64},{64,96},{96,128},{128,160},{160,192},{192,224},{224... | collective-permute-start | bytes 393224 | tf_op jit(solution)/shard_map/ppermute | solution.py:204
  7.6 0.2 shard_map.88.near
  7.9 0.2 collective-permute-done.1.right
  8.1 1.3 %shard_map.89 = f32[16,4,128]{2,1,0:T(4,128)} custom-call(bf16[2,256,128]{2,1,0:T(8,128)(2,1)S(1)} %shard_map.86.both, bf16[2,256,128]{2,1,0:T(8,128)(2,1)S(1)} %collective-permute-done.1.right, f32[2,256,256]{2,1,0:T(8,128)S(1)} %shard_map.88.near), custom_call_target="tpu_custom_call" | custom-call | flops 1 | bytes 1 | tf_op jit(solution)/shard_map/pallas_call | solution.py:215
  9.4 0.0 copy-start.2
  9.4 0.0 copy-start.5
  9.4 13.0 %all-to-all-start = ((f32[16,4,128]{2,1,0:T(4,128)}), f32[16,4,128]{2,1,0:T(4,128)S(1)}, u32[]{:S(2)}, u32[]{:S(2)}) async-start(f32[16,4,128]{2,1,0:T(4,128)} %shard_map.89), calls=%async_computation | async-start | bytes 65536 | tf_op jit(solution)/shard_map/all_to_all | solution.py:223
  22.4 0.0 collective-permute-done.left
  22.4 0.0 copy-done.2
  22.5 0.0 copy-done.5
  22.5 1.7 %shard_map.87 = (bf16[256,128]{1,0:T(8,128)(2,1)}, bf16[256,128]{1,0:T(8,128)(2,1)}, f32[16,256]{1,0:T(8,128)S(1)}) custom-call(bf16[2,256,128]{2,1,0:T(8,128)(2,1)S(1)} %shard_map.86.both, bf16[2,256,128]{2,1,0:T(8,128)(2,1)S(1)} %collective-permute-done.left, bf16[2,256,128]{2,1,0:T(8,128)(2,1)S(1)} %collective-permute-done.1.right, ...), custom_call_target="tpu_custom_call" | custom-call | flops 1 | bytes 1 | tf_op jit(solution)/shard_map/pallas_call | solution.py:225
  24.2 3.3 %all-to-all-done.parts = f32[16,4,128]{2,1,0:T(4,128)S(1)} async-done(((f32[16,4,128]{2,1,0:T(4,128)}), f32[16,4,128]{2,1,0:T(4,128)S(1)}, u32[]{:S(2)}, u32[]{:S(2)}) %all-to-all-start) | async-done | bytes 32800 | tf_op jit(solution)/shard_map/all_to_all | solution.py:223
  27.5 16.4 %all_to_all.10.parts = f32[32,1,4,128]{3,2,1,0:T(4,128)S(1)} all-to-all(f32[32,1,4,128]{3,2,1,0:T(4,128)S(1)} %shard_map.90), channel_id=1, replica_groups={{62,60,58,56,54,52,50,48,46,44,42,40,38,36,34,32,30,28,26,24,22,20,18,1..., dimensions={0} | all-to-all | bytes 131072 | tf_op jit(solution)/shard_map/all_to_all | solution.py:242
  43.9 0.6 %shard_map.91 = f32[16,256]{1,0:T(8,128)} custom-call(f32[32,1,4,128]{3,2,1,0:T(4,128)S(1)} %all_to_all.10.parts, f32[16,256]{1,0:T(8,128)S(1)} %get-tuple-element.12.factor), custom_call_target="tpu_custom_call" | custom-call | flops 1 | bytes 1 | tf_op jit(solution)/shard_map/pallas_call | solution.py:243
  (2 shorter events, 0.0 us)
Async XLA Ops:
  0.6 0.8 %copy-start.1 = (bf16[256,128]{1,0:T(8,128)(2,1)S(1)}, bf16[256,128]{1,0:T(8,128)(2,1)}, u32[]{:S(2)}) copy-start(bf16[256,128]{1,0:T(8,128)(2,1)} %cotangent.1) | copy-start | bytes 196612
  0.6 0.8 %copy-start.3 = (bf16[12,128]{1,0:T(8,128)(2,1)S(1)}, bf16[12,128]{1,0:T(8,128)(2,1)}, u32[]{:S(2)}) copy-start(bf16[12,128]{1,0:T(8,128)(2,1)} %table.1) | copy-start | bytes 9220
  0.7 0.8 %copy-start.4 = (s32[256]{0:T(256)S(1)}, s32[256]{0:T(256)}, u32[]{:S(2)}) copy-start(s32[256]{0:T(256)} %ids.1) | copy-start | bytes 3076
  0.7 0.9 %copy-start = (bf16[256,128]{1,0:T(8,128)(2,1)S(1)}, bf16[256,128]{1,0:T(8,128)(2,1)}, u32[]{:S(2)}) copy-start(bf16[256,128]{1,0:T(8,128)(2,1)} %hidden.1) | copy-start | bytes 196612
  1.8 6.3 %collective-permute-start.1 = (bf16[2,256,128]{2,1,0:T(8,128)(2,1)S(1)}, bf16[2,256,128]{2,1,0:T(8,128)(2,1)S(1)}, u32[]{:S(2)}, u32[]{:S(2)}) collective-permute-start(bf16[2,256,128]{2,1,0:T(8,128)(2,1)S(1)} %shard_map.86.both), channel_id=1, source_target_pairs={{32,0},{64,32},{96,64},{128,96},{160,128},{192,160},{224,192},{256... | collective-permute-start | bytes 393224 | tf_op jit(solution)/shard_map/ppermute | solution.py:205
  3.1 19.4 %collective-permute-start = (bf16[2,256,128]{2,1,0:T(8,128)(2,1)S(1)}, bf16[2,256,128]{2,1,0:T(8,128)(2,1)S(1)}, u32[]{:S(2)}, u32[]{:S(2)}) collective-permute-start(bf16[2,256,128]{2,1,0:T(8,128)(2,1)S(1)} %shard_map.86.both), channel_id=1, source_target_pairs={{0,32},{32,64},{64,96},{96,128},{128,160},{160,192},{192,224},{224... | collective-permute-start | bytes 393224 | tf_op jit(solution)/shard_map/ppermute | solution.py:204
  9.4 13.1 %copy-start.2 = (bf16[16,256]{1,0:T(8,128)(2,1)S(1)}, bf16[16,256]{1,0:T(8,128)(2,1)}, u32[]{:S(2)}) copy-start(bf16[16,256]{1,0:T(8,128)(2,1)} %filters.1) | copy-start | bytes 24580
  9.4 13.1 %copy-start.5 = (s32[16]{0:T(128)S(1)}, s32[16]{0:T(128)}, u32[]{:S(2)}) copy-start(s32[16]{0:T(128)} %lengths.1) | copy-start | bytes 196
  9.4 18.1 %all-to-all-start = ((f32[16,4,128]{2,1,0:T(4,128)}), f32[16,4,128]{2,1,0:T(4,128)S(1)}, u32[]{:S(2)}, u32[]{:S(2)}) async-start(f32[16,4,128]{2,1,0:T(4,128)} %shard_map.89), calls=%async_computation | async-start | bytes 65536 | tf_op jit(solution)/shard_map/all_to_all | solution.py:223

commit v6 on v5

--- a/solution.py
+++ b/solution.py
@@ -18,8 +18,8 @@
 FIRST = ('z', 'core')
 SECOND = ('x_lo', 'x_hi', 'y')
 SIZES = dict(PARTS)
-ORDER1 = list(range(16))[::-1]
-ORDER2 = list(range(32))[::-1]
+ORDER1 = [(i + 12) % 16 for i in range(16)][::-1]
+ORDER2 = [(i + 13) % 32 for i in range(32)][::-1]
 CTX_SIZE = 16
 
 VMEM = pl.BlockSpec(memory_space=pltpu.VMEM)

time: 44.8 us -> 41.2 us (0.920)
  blocking collectives: 16.4 us -> 12.9 us
  waiting for transfers between devices: 3.52 us -> 1.83 us
  starting transfers between devices: 18.9 us -> 20.4 us
    all_to_all x1, blocking collectives: 16.4 us -> 12.9 us  [on_device(): sums = lax.all_to_all(sums, SECOND, 0, 0, axis_index_groups=[ORDER2])]
    all_to_all x1, waiting for transfers between devices: 3.34 us -> 1.65 us  [on_device(): sums = lax.all_to_all(sums, FIRST, 0, 0, axis_index_groups=[ORDER1])]
    all_to_all x1, starting transfers between devices: 13 us -> 14.5 us  [on_device(): sums = lax.all_to_all(sums, FIRST, 0, 0, axis_index_groups=[ORDER1])]
  transfers between devices with their start and end apart: 3 -> 3, of which waited for: 2 -> 2; matrix products, arithmetic and copies ran while one was open for 0% -> 0% of each run, Pallas kernels for 7% -> 8%
where the time goes in v6:
time: 41.2 us; the launch traced here: 40.8 us
  starting transfers between devices  20.4 us (50%)
  blocking collectives  12.9 us (31%)
  Pallas kernels  4.13 us (10%)
  waiting for transfers between devices  1.83 us (4%)
  local copies, waits for them, and re-layouts  0.87 us (2%)
  between operations  0.72 us (2%)
    all_to_all x1, starting transfers between devices, on_device(): sums = lax.all_to_all(sums, FIRST, 0, 0, axis_index_groups=[ORDER1])  14.5 us
    all_to_all x1, blocking collectives, on_device(): sums = lax.all_to_all(sums, SECOND, 0, 0, axis_index_groups=[ORDER2])  12.9 us
    ppermute x1, starting transfers between devices, on_device(): left = lax.ppermute(both, CTX, up)  4.58 us
    pallas_call x1, Pallas kernels, on_device(): pl.pallas_call(outputs_kernel, out_shape=(block, block, shape((GROUPS, TA...  1.69 us
    all_to_all x1, waiting for transfers between devices, on_device(): sums = lax.all_to_all(sums, FIRST, 0, 0, axis_index_groups=[ORDER1])  1.65 us
    pallas_call x1, Pallas kernels, on_device(): pl.pallas_call(correlate_kernel, out_shape=shape((math.prod((SIZES[a] for...  1.34 us
    ppermute x1, starting transfers between devices, on_device(): right = lax.ppermute(both, CTX, [(j, i) for i, j in up])  1.29 us
    unnamed x12, local copies, waits for them, and re-layouts  0.87 us
  transfers between devices with their start and end apart: 3, of which 2 were waited for; matrix products, arithmetic and copies ran while one was open for 0% of the time, Pallas kernels for 8%

profile of v6, /device:TPU:1, one launch (start us, length us, event | category | flops | bytes accessed | tf_op | source)
XLA Modules:
  0.0 40.8 jit_solution(17561765789547862325)
XLA Ops:
  0.6 0.0 copy-start.1
  0.6 0.0 copy-start.3
  0.7 0.0 copy-start.4
  0.7 0.0 copy-start
  0.7 0.8 %copy-done.1 = bf16[256,128]{1,0:T(8,128)(2,1)S(1)} copy-done((bf16[256,128]{1,0:T(8,128)(2,1)S(1)}, bf16[256,128]{1,0:T(8,128)(2,1)}, u32[]{:S(2)}) %copy-start.1) | copy-done | bytes 65560
  1.5 0.0 copy-done.3
  1.5 0.0 copy-done.4
  1.5 0.1 copy-done
  1.5 0.2 shard_map.86.both
  1.8 1.3 %collective-permute-start.1 = (bf16[2,256,128]{2,1,0:T(8,128)(2,1)S(1)}, bf16[2,256,128]{2,1,0:T(8,128)(2,1)S(1)}, u32[]{:S(2)}, u32[]{:S(2)}) collective-permute-start(bf16[2,256,128]{2,1,0:T(8,128)(2,1)S(1)} %shard_map.86.both), channel_id=1, source_target_pairs={{32,0},{64,32},{96,64},{128,96},{160,128},{192,160},{224,192},{256... | collective-permute-start | bytes 393224 | tf_op jit(solution)/shard_map/ppermute | solution.py:205
  3.1 4.6 %collective-permute-start = (bf16[2,256,128]{2,1,0:T(8,128)(2,1)S(1)}, bf16[2,256,128]{2,1,0:T(8,128)(2,1)S(1)}, u32[]{:S(2)}, u32[]{:S(2)}) collective-permute-start(bf16[2,256,128]{2,1,0:T(8,128)(2,1)S(1)} %shard_map.86.both), channel_id=1, source_target_pairs={{0,32},{32,64},{64,96},{96,128},{128,160},{160,192},{192,224},{224... | collective-permute-start | bytes 393224 | tf_op jit(solution)/shard_map/ppermute | solution.py:204
  7.6 0.2 shard_map.88.near
  7.9 0.2 collective-permute-done.1.right
  8.1 1.3 %shard_map.89 = f32[16,4,128]{2,1,0:T(4,128)} custom-call(bf16[2,256,128]{2,1,0:T(8,128)(2,1)S(1)} %shard_map.86.both, bf16[2,256,128]{2,1,0:T(8,128)(2,1)S(1)} %collective-permute-done.1.right, f32[2,256,256]{2,1,0:T(8,128)S(1)} %shard_map.88.near), custom_call_target="tpu_custom_call" | custom-call | flops 1 | bytes 1 | tf_op jit(solution)/shard_map/pallas_call | solution.py:215
  9.4 0.0 copy-start.2
  9.4 0.0 copy-start.5
  9.4 14.5 %all-to-all-start = ((f32[16,4,128]{2,1,0:T(4,128)}), f32[16,4,128]{2,1,0:T(4,128)S(1)}, u32[]{:S(2)}, u32[]{:S(2)}) async-start(f32[16,4,128]{2,1,0:T(4,128)} %shard_map.89), calls=%async_computation | async-start | bytes 65536 | tf_op jit(solution)/shard_map/all_to_all | solution.py:223
  23.9 0.0 collective-permute-done.left
  23.9 0.0 copy-done.2
  23.9 0.0 copy-done.5
  23.9 1.7 %shard_map.87 = (bf16[256,128]{1,0:T(8,128)(2,1)}, bf16[256,128]{1,0:T(8,128)(2,1)}, f32[16,256]{1,0:T(8,128)S(1)}) custom-call(bf16[2,256,128]{2,1,0:T(8,128)(2,1)S(1)} %shard_map.86.both, bf16[2,256,128]{2,1,0:T(8,128)(2,1)S(1)} %collective-permute-done.left, bf16[2,256,128]{2,1,0:T(8,128)(2,1)S(1)} %collective-permute-done.1.right, ...), custom_call_target="tpu_custom_call" | custom-call | flops 1 | bytes 1 | tf_op jit(solution)/shard_map/pallas_call | solution.py:225
  25.6 1.6 %all-to-all-done.parts = f32[16,4,128]{2,1,0:T(4,128)S(1)} async-done(((f32[16,4,128]{2,1,0:T(4,128)}), f32[16,4,128]{2,1,0:T(4,128)S(1)}, u32[]{:S(2)}, u32[]{:S(2)}) %all-to-all-start) | async-done | bytes 32800 | tf_op jit(solution)/shard_map/all_to_all | solution.py:223
  27.3 12.9 %all_to_all.10.parts = f32[32,1,4,128]{3,2,1,0:T(4,128)S(1)} all-to-all(f32[32,1,4,128]{3,2,1,0:T(4,128)S(1)} %shard_map.90), channel_id=1, replica_groups={{24,22,20,18,16,14,12,10,8,6,4,2,0,62,60,58,56,54,52,50,48,46,44,42,40,..., dimensions={0} | all-to-all | bytes 131072 | tf_op jit(solution)/shard_map/all_to_all | solution.py:242
  40.2 0.6 %shard_map.91 = f32[16,256]{1,0:T(8,128)} custom-call(f32[32,1,4,128]{3,2,1,0:T(4,128)S(1)} %all_to_all.10.parts, f32[16,256]{1,0:T(8,128)S(1)} %get-tuple-element.12.factor), custom_call_target="tpu_custom_call" | custom-call | flops 1 | bytes 1 | tf_op jit(solution)/shard_map/pallas_call | solution.py:243
  (2 shorter events, 0.0 us)
Async XLA Ops:
  0.6 0.8 %copy-start.1 = (bf16[256,128]{1,0:T(8,128)(2,1)S(1)}, bf16[256,128]{1,0:T(8,128)(2,1)}, u32[]{:S(2)}) copy-start(bf16[256,128]{1,0:T(8,128)(2,1)} %cotangent.1) | copy-start | bytes 196612
  0.6 0.8 %copy-start.3 = (bf16[12,128]{1,0:T(8,128)(2,1)S(1)}, bf16[12,128]{1,0:T(8,128)(2,1)}, u32[]{:S(2)}) copy-start(bf16[12,128]{1,0:T(8,128)(2,1)} %table.1) | copy-start | bytes 9220
  0.7 0.8 %copy-start.4 = (s32[256]{0:T(256)S(1)}, s32[256]{0:T(256)}, u32[]{:S(2)}) copy-start(s32[256]{0:T(256)} %ids.1) | copy-start | bytes 3076
  0.7 0.9 %copy-start = (bf16[256,128]{1,0:T(8,128)(2,1)S(1)}, bf16[256,128]{1,0:T(8,128)(2,1)}, u32[]{:S(2)}) copy-start(bf16[256,128]{1,0:T(8,128)(2,1)} %hidden.1) | copy-start | bytes 196612
  1.8 6.3 %collective-permute-start.1 = (bf16[2,256,128]{2,1,0:T(8,128)(2,1)S(1)}, bf16[2,256,128]{2,1,0:T(8,128)(2,1)S(1)}, u32[]{:S(2)}, u32[]{:S(2)}) collective-permute-start(bf16[2,256,128]{2,1,0:T(8,128)(2,1)S(1)} %shard_map.86.both), channel_id=1, source_target_pairs={{32,0},{64,32},{96,64},{128,96},{160,128},{192,160},{224,192},{256... | collective-permute-start | bytes 393224 | tf_op jit(solution)/shard_map/ppermute | solution.py:205
  3.1 20.8 %collective-permute-start = (bf16[2,256,128]{2,1,0:T(8,128)(2,1)S(1)}, bf16[2,256,128]{2,1,0:T(8,128)(2,1)S(1)}, u32[]{:S(2)}, u32[]{:S(2)}) collective-permute-start(bf16[2,256,128]{2,1,0:T(8,128)(2,1)S(1)} %shard_map.86.both), channel_id=1, source_target_pairs={{0,32},{32,64},{64,96},{96,128},{128,160},{160,192},{192,224},{224... | collective-permute-start | bytes 393224 | tf_op jit(solution)/shard_map/ppermute | solution.py:204
  9.4 14.5 %copy-start.2 = (bf16[16,256]{1,0:T(8,128)(2,1)S(1)}, bf16[16,256]{1,0:T(8,128)(2,1)}, u32[]{:S(2)}) copy-start(bf16[16,256]{1,0:T(8,128)(2,1)} %filters.1) | copy-start | bytes 24580
  9.4 14.5 %copy-start.5 = (s32[16]{0:T(128)S(1)}, s32[16]{0:T(128)}, u32[]{:S(2)}) copy-start(s32[16]{0:T(128)} %lengths.1) | copy-start | bytes 196
  9.4 17.9 %all-to-all-start = ((f32[16,4,128]{2,1,0:T(4,128)}), f32[16,4,128]{2,1,0:T(4,128)S(1)}, u32[]{:S(2)}, u32[]{:S(2)}) async-start(f32[16,4,128]{2,1,0:T(4,128)} %shard_map.89), calls=%async_computation | async-start | bytes 65536 | tf_op jit(solution)/shard_map/all_to_all | solution.py:223

commit v7 on v6

--- a/solution.py
+++ b/solution.py
@@ -54,13 +54,16 @@
 
 
 def lag_sums(product):
-    half = ROWS // 2
-    while half >= 8:
-        product = product[:half] + pltpu.roll(product[half:], TAPS - half, 1)
-        half //= 2
+    for rows, parts in ((64, 4), (16, 4), (8, 2)):
+        pieces = [product[:rows]]
+        for part in range(1, parts):
+            piece = product[part * rows : (part + 1) * rows]
+            pieces.append(pltpu.roll(piece, TAPS - part * rows, 1))
+        product = tree_sum(pieces)
     row = iota(product.shape, 0)
-    for step in (4, 2, 1):
-        product = jnp.where((row & step) != 0, pltpu.roll(product, TAPS - step, 1), product)
+    rolled = [pltpu.roll(product, TAPS - step, 1) for step in range(1, 8)]
+    for step, piece in enumerate(rolled, 1):
+        product = jnp.where(row == step, piece, product)
     return jnp.sum(product, axis=0, keepdims=True)
 
 

time: 41.2 us -> 41.1 us (level)
  no operation moved by 1% of the time
where the time goes in v7:
time: 41.1 us; the launch traced here: 40.7 us
  starting transfers between devices  20.4 us (50%)
  blocking collectives  12.9 us (31%)
  Pallas kernels  3.94 us (10%)
  waiting for transfers between devices  1.83 us (4%)
  local copies, waits for them, and re-layouts  0.87 us (2%)
  between operations  0.72 us (2%)
    all_to_all x1, starting transfers between devices, on_device(): sums = lax.all_to_all(sums, FIRST, 0, 0, axis_index_groups=[ORDER1])  14.5 us
    all_to_all x1, blocking collectives, on_device(): sums = lax.all_to_all(sums, SECOND, 0, 0, axis_index_groups=[ORDER2])  12.9 us
    ppermute x1, starting transfers between devices, on_device(): left = lax.ppermute(both, CTX, up)  4.58 us
    pallas_call x1, Pallas kernels, on_device(): pl.pallas_call(outputs_kernel, out_shape=(block, block, shape((GROUPS, TA...  1.69 us
    all_to_all x1, waiting for transfers between devices, on_device(): sums = lax.all_to_all(sums, FIRST, 0, 0, axis_index_groups=[ORDER1])  1.65 us
    ppermute x1, starting transfers between devices, on_device(): right = lax.ppermute(both, CTX, [(j, i) for i, j in up])  1.29 us
    pallas_call x1, Pallas kernels, on_device(): pl.pallas_call(correlate_kernel, out_shape=shape((math.prod((SIZES[a] for...  1.16 us
    unnamed x12, local copies, waits for them, and re-layouts  0.87 us
  transfers between devices with their start and end apart: 3, of which 2 were waited for; matrix products, arithmetic and copies ran while one was open for 0% of the time, Pallas kernels for 8%

profile of v7, /device:TPU:1, one launch (start us, length us, event | category | flops | bytes accessed | tf_op | source)
XLA Modules:
  0.0 40.7 jit_solution(3686947679324273781)
XLA Ops:
  0.6 0.0 copy-start.1
  0.6 0.0 copy-start.3
  0.7 0.0 copy-start.4
  0.7 0.0 copy-start
  0.7 0.8 %copy-done.1 = bf16[256,128]{1,0:T(8,128)(2,1)S(1)} copy-done((bf16[256,128]{1,0:T(8,128)(2,1)S(1)}, bf16[256,128]{1,0:T(8,128)(2,1)}, u32[]{:S(2)}) %copy-start.1) | copy-done | bytes 65560
  1.5 0.0 copy-done.3
  1.5 0.0 copy-done.4
  1.5 0.1 copy-done
  1.5 0.2 shard_map.86.both
  1.8 1.3 %collective-permute-start.1 = (bf16[2,256,128]{2,1,0:T(8,128)(2,1)S(1)}, bf16[2,256,128]{2,1,0:T(8,128)(2,1)S(1)}, u32[]{:S(2)}, u32[]{:S(2)}) collective-permute-start(bf16[2,256,128]{2,1,0:T(8,128)(2,1)S(1)} %shard_map.86.both), channel_id=1, source_target_pairs={{32,0},{64,32},{96,64},{128,96},{160,128},{192,160},{224,192},{256... | collective-permute-start | bytes 393224 | tf_op jit(solution)/shard_map/ppermute | solution.py:208
  3.1 4.6 %collective-permute-start = (bf16[2,256,128]{2,1,0:T(8,128)(2,1)S(1)}, bf16[2,256,128]{2,1,0:T(8,128)(2,1)S(1)}, u32[]{:S(2)}, u32[]{:S(2)}) collective-permute-start(bf16[2,256,128]{2,1,0:T(8,128)(2,1)S(1)} %shard_map.86.both), channel_id=1, source_target_pairs={{0,32},{32,64},{64,96},{96,128},{128,160},{160,192},{192,224},{224... | collective-permute-start | bytes 393224 | tf_op jit(solution)/shard_map/ppermute | solution.py:207
  7.6 0.2 shard_map.88.near
  7.9 0.2 collective-permute-done.1.right
  8.1 1.2 %shard_map.89 = f32[16,4,128]{2,1,0:T(4,128)} custom-call(bf16[2,256,128]{2,1,0:T(8,128)(2,1)S(1)} %shard_map.86.both, bf16[2,256,128]{2,1,0:T(8,128)(2,1)S(1)} %collective-permute-done.1.right, f32[2,256,256]{2,1,0:T(8,128)S(1)} %shard_map.88.near), custom_call_target="tpu_custom_call" | custom-call | flops 1 | bytes 1 | tf_op jit(solution)/shard_map/pallas_call | solution.py:218
  9.2 0.0 copy-start.2
  9.2 0.0 copy-start.5
  9.2 14.5 %all-to-all-start = ((f32[16,4,128]{2,1,0:T(4,128)}), f32[16,4,128]{2,1,0:T(4,128)S(1)}, u32[]{:S(2)}, u32[]{:S(2)}) async-start(f32[16,4,128]{2,1,0:T(4,128)} %shard_map.89), calls=%async_computation | async-start | bytes 65536 | tf_op jit(solution)/shard_map/all_to_all | solution.py:226
  23.7 0.0 collective-permute-done.left
  23.7 0.0 copy-done.2
  23.7 0.0 copy-done.5
  23.7 1.7 %shard_map.87 = (bf16[256,128]{1,0:T(8,128)(2,1)}, bf16[256,128]{1,0:T(8,128)(2,1)}, f32[16,256]{1,0:T(8,128)S(1)}) custom-call(bf16[2,256,128]{2,1,0:T(8,128)(2,1)S(1)} %shard_map.86.both, bf16[2,256,128]{2,1,0:T(8,128)(2,1)S(1)} %collective-permute-done.left, bf16[2,256,128]{2,1,0:T(8,128)(2,1)S(1)} %collective-permute-done.1.right, ...), custom_call_target="tpu_custom_call" | custom-call | flops 1 | bytes 1 | tf_op jit(solution)/shard_map/pallas_call | solution.py:228
  25.4 1.6 %all-to-all-done.parts = f32[16,4,128]{2,1,0:T(4,128)S(1)} async-done(((f32[16,4,128]{2,1,0:T(4,128)}), f32[16,4,128]{2,1,0:T(4,128)S(1)}, u32[]{:S(2)}, u32[]{:S(2)}) %all-to-all-start) | async-done | bytes 32800 | tf_op jit(solution)/shard_map/all_to_all | solution.py:226
  27.1 12.9 %all_to_all.10.parts = f32[32,1,4,128]{3,2,1,0:T(4,128)S(1)} all-to-all(f32[32,1,4,128]{3,2,1,0:T(4,128)S(1)} %shard_map.90), channel_id=1, replica_groups={{24,22,20,18,16,14,12,10,8,6,4,2,0,62,60,58,56,54,52,50,48,46,44,42,40,..., dimensions={0} | all-to-all | bytes 131072 | tf_op jit(solution)/shard_map/all_to_all | solution.py:245
  40.0 0.6 %shard_map.91 = f32[16,256]{1,0:T(8,128)} custom-call(f32[32,1,4,128]{3,2,1,0:T(4,128)S(1)} %all_to_all.10.parts, f32[16,256]{1,0:T(8,128)S(1)} %get-tuple-element.12.factor), custom_call_target="tpu_custom_call" | custom-call | flops 1 | bytes 1 | tf_op jit(solution)/shard_map/pallas_call | solution.py:246
  (2 shorter events, 0.0 us)
Async XLA Ops:
  0.6 0.8 %copy-start.1 = (bf16[256,128]{1,0:T(8,128)(2,1)S(1)}, bf16[256,128]{1,0:T(8,128)(2,1)}, u32[]{:S(2)}) copy-start(bf16[256,128]{1,0:T(8,128)(2,1)} %cotangent.1) | copy-start | bytes 196612
  0.6 0.8 %copy-start.3 = (bf16[12,128]{1,0:T(8,128)(2,1)S(1)}, bf16[12,128]{1,0:T(8,128)(2,1)}, u32[]{:S(2)}) copy-start(bf16[12,128]{1,0:T(8,128)(2,1)} %table.1) | copy-start | bytes 9220
  0.7 0.8 %copy-start.4 = (s32[256]{0:T(256)S(1)}, s32[256]{0:T(256)}, u32[]{:S(2)}) copy-start(s32[256]{0:T(256)} %ids.1) | copy-start | bytes 3076
  0.7 0.9 %copy-start = (bf16[256,128]{1,0:T(8,128)(2,1)S(1)}, bf16[256,128]{1,0:T(8,128)(2,1)}, u32[]{:S(2)}) copy-start(bf16[256,128]{1,0:T(8,128)(2,1)} %hidden.1) | copy-start | bytes 196612
  1.8 6.3 %collective-permute-start.1 = (bf16[2,256,128]{2,1,0:T(8,128)(2,1)S(1)}, bf16[2,256,128]{2,1,0:T(8,128)(2,1)S(1)}, u32[]{:S(2)}, u32[]{:S(2)}) collective-permute-start(bf16[2,256,128]{2,1,0:T(8,128)(2,1)S(1)} %shard_map.86.both), channel_id=1, source_target_pairs={{32,0},{64,32},{96,64},{128,96},{160,128},{192,160},{224,192},{256... | collective-permute-start | bytes 393224 | tf_op jit(solution)/shard_map/ppermute | solution.py:208
  3.1 20.7 %collective-permute-start = (bf16[2,256,128]{2,1,0:T(8,128)(2,1)S(1)}, bf16[2,256,128]{2,1,0:T(8,128)(2,1)S(1)}, u32[]{:S(2)}, u32[]{:S(2)}) collective-permute-start(bf16[2,256,128]{2,1,0:T(8,128)(2,1)S(1)} %shard_map.86.both), channel_id=1, source_target_pairs={{0,32},{32,64},{64,96},{96,128},{128,160},{160,192},{192,224},{224... | collective-permute-start | bytes 393224 | tf_op jit(solution)/shard_map/ppermute | solution.py:207
  9.2 14.5 %copy-start.2 = (bf16[16,256]{1,0:T(8,128)(2,1)S(1)}, bf16[16,256]{1,0:T(8,128)(2,1)}, u32[]{:S(2)}) copy-start(bf16[16,256]{1,0:T(8,128)(2,1)} %filters.1) | copy-start | bytes 24580
  9.2 14.5 %copy-start.5 = (s32[16]{0:T(128)S(1)}, s32[16]{0:T(128)}, u32[]{:S(2)}) copy-start(s32[16]{0:T(128)} %lengths.1) | copy-start | bytes 196
  9.2 17.9 %all-to-all-start = ((f32[16,4,128]{2,1,0:T(4,128)}), f32[16,4,128]{2,1,0:T(4,128)S(1)}, u32[]{:S(2)}, u32[]{:S(2)}) async-start(f32[16,4,128]{2,1,0:T(4,128)} %shard_map.89), calls=%async_computation | async-start | bytes 65536 | tf_op jit(solution)/shard_map/all_to_all | solution.py:226

commit v8 on v7

--- a/solution.py
+++ b/solution.py
@@ -53,13 +53,17 @@
     both[1] = cotangent[...]
 
 
-def lag_sums(product):
+def fold_rows(product):
     for rows, parts in ((64, 4), (16, 4), (8, 2)):
         pieces = [product[:rows]]
         for part in range(1, parts):
             piece = product[part * rows : (part + 1) * rows]
             pieces.append(pltpu.roll(piece, TAPS - part * rows, 1))
         product = tree_sum(pieces)
+    return product
+
+
+def lag_sums(product):
     row = iota(product.shape, 0)
     rolled = [pltpu.roll(product, TAPS - step, 1) for step in range(1, 8)]
     for step, piece in enumerate(rolled, 1):
@@ -78,7 +82,7 @@
 def near_kernel(both, near):
     here = lag_here()
     for first, second in ((0, 1), (1, 0)):
-        near[first] = jnp.where(here, dot(both[first], both[second], LANE), 0.0)
+        near[first] = fold_rows(jnp.where(here, dot(both[first], both[second], LANE), 0.0))
 
 
 def correlate_kernel(both, right, near, out):
@@ -86,7 +90,7 @@
     sums = []
     for first, second in ((0, 1), (1, 0)):
         far = dot(both[first], right[second], LANE)
-        sums.append(lag_sums(jnp.where(here, near[first], far)))
+        sums.append(lag_sums(fold_rows(jnp.where(here, 0.0, far)) + near[first]))
     half = TAPS // 2
     pieces = [sums[0][:, :half], sums[0][:, half:], sums[1][:, :half], sums[1][:, half:]]
     row = iota((4, half), 0)
@@ -206,7 +210,7 @@
     up = [(i, i + 1) for i in range(CTX_SIZE - 1)]
     left = lax.ppermute(both, CTX, up)
     right = lax.ppermute(both, CTX, [(j, i) for i, j in up])
-    pair = (2, ROWS, ROWS)
+    pair = (2, 8, ROWS)
     near = pl.pallas_call(
         near_kernel,
         out_shape=shape(pair, jnp.float32),

time: 41.1 us -> 41 us (level)
  transfers between devices with their start and end apart: 3 -> 3, of which waited for: 2 -> 1; matrix products, arithmetic and copies ran while one was open for 0% -> 0% of each run, Pallas kernels for 8% -> 8%
where the time goes in v8:
time: 41 us; the launch traced here: 40.6 us
  starting transfers between devices  20.3 us (50%)
  blocking collectives  12.9 us (31%)
  Pallas kernels  4.16 us (10%)
  waiting for transfers between devices  1.65 us (4%)
  local copies, waits for them, and re-layouts  0.84 us (2%)
  between operations  0.71 us (2%)
    all_to_all x1, starting transfers between devices, on_device(): sums = lax.all_to_all(sums, FIRST, 0, 0, axis_index_groups=[ORDER1])  14.4 us
    all_to_all x1, blocking collectives, on_device(): sums = lax.all_to_all(sums, SECOND, 0, 0, axis_index_groups=[ORDER2])  12.9 us
    ppermute x1, starting transfers between devices, on_device(): left = lax.ppermute(both, CTX, up)  4.58 us
    pallas_call x1, Pallas kernels, on_device(): pl.pallas_call(outputs_kernel, out_shape=(block, block, shape((GROUPS, TA...  1.69 us
    all_to_all x1, waiting for transfers between devices, on_device(): sums = lax.all_to_all(sums, FIRST, 0, 0, axis_index_groups=[ORDER1])  1.65 us
    ppermute x1, starting transfers between devices, on_device(): right = lax.ppermute(both, CTX, [(j, i) for i, j in up])  1.29 us
    pallas_call x1, Pallas kernels, on_device(): pl.pallas_call(correlate_kernel, out_shape=shape((math.prod((SIZES[a] for...  1.17 us
    unnamed x12, local copies, waits for them, and re-layouts  0.84 us
  transfers between devices with their start and end apart: 3, of which 1 were waited for; matrix products, arithmetic and copies ran while one was open for 0% of the time, Pallas kernels for 8%

profile of v8, /device:TPU:1, one launch (start us, length us, event | category | flops | bytes accessed | tf_op | source)
XLA Modules:
  0.0 40.6 jit_solution(9766149627911173988)
XLA Ops:
  0.6 0.0 copy-start.1
  0.6 0.0 copy-start
  0.7 0.0 copy-start.4
  0.7 0.0 copy-start.3
  0.7 0.8 %copy-done.1 = bf16[256,128]{1,0:T(8,128)(2,1)S(1)} copy-done((bf16[256,128]{1,0:T(8,128)(2,1)S(1)}, bf16[256,128]{1,0:T(8,128)(2,1)}, u32[]{:S(2)}) %copy-start.1) | copy-done | bytes 65560
  1.5 0.0 copy-done
  1.5 0.0 copy-done.4
  1.5 0.0 copy-done.3
  1.5 0.2 shard_map.86.both
  1.7 1.3 %collective-permute-start.1 = (bf16[2,256,128]{2,1,0:T(8,128)(2,1)S(1)}, bf16[2,256,128]{2,1,0:T(8,128)(2,1)S(1)}, u32[]{:S(2)}, u32[]{:S(2)}) collective-permute-start(bf16[2,256,128]{2,1,0:T(8,128)(2,1)S(1)} %shard_map.86.both), channel_id=1, source_target_pairs={{32,0},{64,32},{96,64},{128,96},{160,128},{192,160},{224,192},{256... | collective-permute-start | bytes 393224 | tf_op jit(solution)/shard_map/ppermute | solution.py:212
  3.0 4.6 %collective-permute-start = (bf16[2,256,128]{2,1,0:T(8,128)(2,1)S(1)}, bf16[2,256,128]{2,1,0:T(8,128)(2,1)S(1)}, u32[]{:S(2)}, u32[]{:S(2)}) collective-permute-start(bf16[2,256,128]{2,1,0:T(8,128)(2,1)S(1)} %shard_map.86.both), channel_id=1, source_target_pairs={{0,32},{32,64},{64,96},{96,128},{128,160},{160,192},{192,224},{224... | collective-permute-start | bytes 393224 | tf_op jit(solution)/shard_map/ppermute | solution.py:211
  7.6 0.4 %shard_map.88.near = f32[2,8,256]{2,1,0:T(8,128)S(1)} custom-call(bf16[2,256,128]{2,1,0:T(8,128)(2,1)S(1)} %shard_map.86.both), custom_call_target="tpu_custom_call" | custom-call | flops 1 | bytes 1 | tf_op jit(solution)/shard_map/pallas_call | solution.py:214
  8.1 0.0 collective-permute-done.1.right
  8.1 1.2 %shard_map.89 = f32[16,4,128]{2,1,0:T(4,128)} custom-call(bf16[2,256,128]{2,1,0:T(8,128)(2,1)S(1)} %shard_map.86.both, bf16[2,256,128]{2,1,0:T(8,128)(2,1)S(1)} %collective-permute-done.1.right, f32[2,8,256]{2,1,0:T(8,128)S(1)} %shard_map.88.near), custom_call_target="tpu_custom_call" | custom-call | flops 1 | bytes 1 | tf_op jit(solution)/shard_map/pallas_call | solution.py:222
  9.2 0.0 copy-start.2
  9.2 0.0 copy-start.5
  9.2 14.4 %all-to-all-start = ((f32[16,4,128]{2,1,0:T(4,128)}), f32[16,4,128]{2,1,0:T(4,128)S(1)}, u32[]{:S(2)}, u32[]{:S(2)}) async-start(f32[16,4,128]{2,1,0:T(4,128)} %shard_map.89), calls=%async_computation | async-start | bytes 65536 | tf_op jit(solution)/shard_map/all_to_all | solution.py:230
  23.7 0.0 collective-permute-done.left
  23.7 0.0 copy-done.2
  23.7 0.0 copy-done.5
  23.7 1.7 %shard_map.87 = (bf16[256,128]{1,0:T(8,128)(2,1)}, bf16[256,128]{1,0:T(8,128)(2,1)}, f32[16,256]{1,0:T(8,128)S(1)}) custom-call(bf16[2,256,128]{2,1,0:T(8,128)(2,1)S(1)} %shard_map.86.both, bf16[2,256,128]{2,1,0:T(8,128)(2,1)S(1)} %collective-permute-done.left, bf16[2,256,128]{2,1,0:T(8,128)(2,1)S(1)} %collective-permute-done.1.right, ...), custom_call_target="tpu_custom_call" | custom-call | flops 1 | bytes 1 | tf_op jit(solution)/shard_map/pallas_call | solution.py:232
  25.4 1.6 %all-to-all-done.parts = f32[16,4,128]{2,1,0:T(4,128)S(1)} async-done(((f32[16,4,128]{2,1,0:T(4,128)}), f32[16,4,128]{2,1,0:T(4,128)S(1)}, u32[]{:S(2)}, u32[]{:S(2)}) %all-to-all-start) | async-done | bytes 32800 | tf_op jit(solution)/shard_map/all_to_all | solution.py:230
  27.1 12.9 %all_to_all.10.parts = f32[32,1,4,128]{3,2,1,0:T(4,128)S(1)} all-to-all(f32[32,1,4,128]{3,2,1,0:T(4,128)S(1)} %shard_map.90), channel_id=1, replica_groups={{24,22,20,18,16,14,12,10,8,6,4,2,0,62,60,58,56,54,52,50,48,46,44,42,40,..., dimensions={0} | all-to-all | bytes 131072 | tf_op jit(solution)/shard_map/all_to_all | solution.py:249
  40.0 0.6 %shard_map.91 = f32[16,256]{1,0:T(8,128)} custom-call(f32[32,1,4,128]{3,2,1,0:T(4,128)S(1)} %all_to_all.10.parts, f32[16,256]{1,0:T(8,128)S(1)} %get-tuple-element.12.factor), custom_call_target="tpu_custom_call" | custom-call | flops 1 | bytes 1 | tf_op jit(solution)/shard_map/pallas_call | solution.py:250
  (2 shorter events, 0.0 us)
Async XLA Ops:
  0.6 0.8 %copy-start.1 = (bf16[256,128]{1,0:T(8,128)(2,1)S(1)}, bf16[256,128]{1,0:T(8,128)(2,1)}, u32[]{:S(2)}) copy-start(bf16[256,128]{1,0:T(8,128)(2,1)} %cotangent.1) | copy-start | bytes 196612
  0.6 0.9 %copy-start = (bf16[256,128]{1,0:T(8,128)(2,1)S(1)}, bf16[256,128]{1,0:T(8,128)(2,1)}, u32[]{:S(2)}) copy-start(bf16[256,128]{1,0:T(8,128)(2,1)} %hidden.1) | copy-start | bytes 196612
  0.7 0.9 %copy-start.4 = (s32[256]{0:T(256)S(1)}, s32[256]{0:T(256)}, u32[]{:S(2)}) copy-start(s32[256]{0:T(256)} %ids.1) | copy-start | bytes 3076
  0.7 0.8 %copy-start.3 = (bf16[12,128]{1,0:T(8,128)(2,1)S(1)}, bf16[12,128]{1,0:T(8,128)(2,1)}, u32[]{:S(2)}) copy-start(bf16[12,128]{1,0:T(8,128)(2,1)} %table.1) | copy-start | bytes 9220
  1.7 6.3 %collective-permute-start.1 = (bf16[2,256,128]{2,1,0:T(8,128)(2,1)S(1)}, bf16[2,256,128]{2,1,0:T(8,128)(2,1)S(1)}, u32[]{:S(2)}, u32[]{:S(2)}) collective-permute-start(bf16[2,256,128]{2,1,0:T(8,128)(2,1)S(1)} %shard_map.86.both), channel_id=1, source_target_pairs={{32,0},{64,32},{96,64},{128,96},{160,128},{192,160},{224,192},{256... | collective-permute-start | bytes 393224 | tf_op jit(solution)/shard_map/ppermute | solution.py:212
  3.0 20.7 %collective-permute-start = (bf16[2,256,128]{2,1,0:T(8,128)(2,1)S(1)}, bf16[2,256,128]{2,1,0:T(8,128)(2,1)S(1)}, u32[]{:S(2)}, u32[]{:S(2)}) collective-permute-start(bf16[2,256,128]{2,1,0:T(8,128)(2,1)S(1)} %shard_map.86.both), channel_id=1, source_target_pairs={{0,32},{32,64},{64,96},{96,128},{128,160},{160,192},{192,224},{224... | collective-permute-start | bytes 393224 | tf_op jit(solution)/shard_map/ppermute | solution.py:211
  9.2 14.5 %copy-start.2 = (bf16[16,256]{1,0:T(8,128)(2,1)S(1)}, bf16[16,256]{1,0:T(8,128)(2,1)}, u32[]{:S(2)}) copy-start(bf16[16,256]{1,0:T(8,128)(2,1)} %filters.1) | copy-start | bytes 24580
  9.2 14.5 %copy-start.5 = (s32[16]{0:T(128)S(1)}, s32[16]{0:T(128)}, u32[]{:S(2)}) copy-start(s32[16]{0:T(128)} %lengths.1) | copy-start | bytes 196
  9.2 17.8 %all-to-all-start = ((f32[16,4,128]{2,1,0:T(4,128)}), f32[16,4,128]{2,1,0:T(4,128)S(1)}, u32[]{:S(2)}, u32[]{:S(2)}) async-start(f32[16,4,128]{2,1,0:T(4,128)} %shard_map.89), calls=%async_computation | async-start | bytes 65536 | tf_op jit(solution)/shard_map/all_to_all | solution.py:230

commit v9 on v8

--- a/solution.py
+++ b/solution.py
@@ -18,7 +18,7 @@
 FIRST = ('z', 'core')
 SECOND = ('x_lo', 'x_hi', 'y')
 SIZES = dict(PARTS)
-ORDER1 = [(i + 12) % 16 for i in range(16)][::-1]
+ORDER1 = [(i + 10) % 16 for i in range(16)][::-1]
 ORDER2 = [(i + 13) % 32 for i in range(32)][::-1]
 CTX_SIZE = 16
 

time: 41 us -> 41 us (level)
  starting transfers between devices: 20.3 us -> 21.2 us
  waiting for transfers between devices: 1.65 us -> 0.8 us
    all_to_all x1, starting transfers between devices: 14.4 us -> 15.3 us  [on_device(): sums = lax.all_to_all(sums, FIRST, 0, 0, axis_index_groups=[ORDER1])]
    all_to_all x1, waiting for transfers between devices: 1.65 us -> 0.8 us  [on_device(): sums = lax.all_to_all(sums, FIRST, 0, 0, axis_index_groups=[ORDER1])]
where the time goes in v9:
time: 41 us; the launch traced here: 40.7 us
  starting transfers between devices  21.2 us (52%)
  blocking collectives  12.9 us (31%)
  Pallas kernels  4.17 us (10%)
  local copies, waits for them, and re-layouts  0.84 us (2%)
  waiting for transfers between devices  0.8 us (2%)
  between operations  0.71 us (2%)
    all_to_all x1, starting transfers between devices, on_device(): sums = lax.all_to_all(sums, FIRST, 0, 0, axis_index_groups=[ORDER1])  15.3 us
    all_to_all x1, blocking collectives, on_device(): sums = lax.all_to_all(sums, SECOND, 0, 0, axis_index_groups=[ORDER2])  12.9 us
    ppermute x1, starting transfers between devices, on_device(): left = lax.ppermute(both, CTX, up)  4.58 us
    pallas_call x1, Pallas kernels, on_device(): pl.pallas_call(outputs_kernel, out_shape=(block, block, shape((GROUPS, TA...  1.69 us
    ppermute x1, starting transfers between devices, on_device(): right = lax.ppermute(both, CTX, [(j, i) for i, j in up])  1.29 us
    pallas_call x1, Pallas kernels, on_device(): pl.pallas_call(correlate_kernel, out_shape=shape((math.prod((SIZES[a] for...  1.17 us
    unnamed x12, local copies, waits for them, and re-layouts  0.84 us
  transfers between devices with their start and end apart: 3, of which 1 were waited for; matrix products, arithmetic and copies ran while one was open for 0% of the time, Pallas kernels for 8%

profile of v9, /device:TPU:1, one launch (start us, length us, event | category | flops | bytes accessed | tf_op | source)
XLA Modules:
  0.0 40.7 jit_solution(3530284970737259681)
XLA Ops:
  0.6 0.0 copy-start.1
  0.6 0.0 copy-start
  0.7 0.0 copy-start.4
  0.7 0.0 copy-start.3
  0.7 0.8 %copy-done.1 = bf16[256,128]{1,0:T(8,128)(2,1)S(1)} copy-done((bf16[256,128]{1,0:T(8,128)(2,1)S(1)}, bf16[256,128]{1,0:T(8,128)(2,1)}, u32[]{:S(2)}) %copy-start.1) | copy-done | bytes 65560
  1.5 0.0 copy-done
  1.5 0.0 copy-done.4
  1.5 0.0 copy-done.3
  1.5 0.2 shard_map.86.both
  1.7 1.3 %collective-permute-start.1 = (bf16[2,256,128]{2,1,0:T(8,128)(2,1)S(1)}, bf16[2,256,128]{2,1,0:T(8,128)(2,1)S(1)}, u32[]{:S(2)}, u32[]{:S(2)}) collective-permute-start(bf16[2,256,128]{2,1,0:T(8,128)(2,1)S(1)} %shard_map.86.both), channel_id=1, source_target_pairs={{32,0},{64,32},{96,64},{128,96},{160,128},{192,160},{224,192},{256... | collective-permute-start | bytes 393224 | tf_op jit(solution)/shard_map/ppermute | solution.py:212
  3.0 4.6 %collective-permute-start = (bf16[2,256,128]{2,1,0:T(8,128)(2,1)S(1)}, bf16[2,256,128]{2,1,0:T(8,128)(2,1)S(1)}, u32[]{:S(2)}, u32[]{:S(2)}) collective-permute-start(bf16[2,256,128]{2,1,0:T(8,128)(2,1)S(1)} %shard_map.86.both), channel_id=1, source_target_pairs={{0,32},{32,64},{64,96},{96,128},{128,160},{160,192},{192,224},{224... | collective-permute-start | bytes 393224 | tf_op jit(solution)/shard_map/ppermute | solution.py:211
  7.6 0.4 %shard_map.88.near = f32[2,8,256]{2,1,0:T(8,128)S(1)} custom-call(bf16[2,256,128]{2,1,0:T(8,128)(2,1)S(1)} %shard_map.86.both), custom_call_target="tpu_custom_call" | custom-call | flops 1 | bytes 1 | tf_op jit(solution)/shard_map/pallas_call | solution.py:214
  8.1 0.0 collective-permute-done.1.right
  8.1 1.2 %shard_map.89 = f32[16,4,128]{2,1,0:T(4,128)} custom-call(bf16[2,256,128]{2,1,0:T(8,128)(2,1)S(1)} %shard_map.86.both, bf16[2,256,128]{2,1,0:T(8,128)(2,1)S(1)} %collective-permute-done.1.right, f32[2,8,256]{2,1,0:T(8,128)S(1)} %shard_map.88.near), custom_call_target="tpu_custom_call" | custom-call | flops 1 | bytes 1 | tf_op jit(solution)/shard_map/pallas_call | solution.py:222
  9.2 0.0 copy-start.2
  9.2 0.0 copy-start.5
  9.2 15.3 %all-to-all-start = ((f32[16,4,128]{2,1,0:T(4,128)}), f32[16,4,128]{2,1,0:T(4,128)S(1)}, u32[]{:S(2)}, u32[]{:S(2)}) async-start(f32[16,4,128]{2,1,0:T(4,128)} %shard_map.89), calls=%async_computation | async-start | bytes 65536 | tf_op jit(solution)/shard_map/all_to_all | solution.py:230
  24.6 0.0 collective-permute-done.left
  24.6 0.0 copy-done.2
  24.6 0.0 copy-done.5
  24.6 1.7 %shard_map.87 = (bf16[256,128]{1,0:T(8,128)(2,1)}, bf16[256,128]{1,0:T(8,128)(2,1)}, f32[16,256]{1,0:T(8,128)S(1)}) custom-call(bf16[2,256,128]{2,1,0:T(8,128)(2,1)S(1)} %shard_map.86.both, bf16[2,256,128]{2,1,0:T(8,128)(2,1)S(1)} %collective-permute-done.left, bf16[2,256,128]{2,1,0:T(8,128)(2,1)S(1)} %collective-permute-done.1.right, ...), custom_call_target="tpu_custom_call" | custom-call | flops 1 | bytes 1 | tf_op jit(solution)/shard_map/pallas_call | solution.py:232
  26.3 0.8 %all-to-all-done.parts = f32[16,4,128]{2,1,0:T(4,128)S(1)} async-done(((f32[16,4,128]{2,1,0:T(4,128)}), f32[16,4,128]{2,1,0:T(4,128)S(1)}, u32[]{:S(2)}, u32[]{:S(2)}) %all-to-all-start) | async-done | bytes 32800 | tf_op jit(solution)/shard_map/all_to_all | solution.py:230
  27.1 12.9 %all_to_all.10.parts = f32[32,1,4,128]{3,2,1,0:T(4,128)S(1)} all-to-all(f32[32,1,4,128]{3,2,1,0:T(4,128)S(1)} %shard_map.90), channel_id=1, replica_groups={{24,22,20,18,16,14,12,10,8,6,4,2,0,62,60,58,56,54,52,50,48,46,44,42,40,..., dimensions={0} | all-to-all | bytes 131072 | tf_op jit(solution)/shard_map/all_to_all | solution.py:249
  40.1 0.6 %shard_map.91 = f32[16,256]{1,0:T(8,128)} custom-call(f32[32,1,4,128]{3,2,1,0:T(4,128)S(1)} %all_to_all.10.parts, f32[16,256]{1,0:T(8,128)S(1)} %get-tuple-element.12.factor), custom_call_target="tpu_custom_call" | custom-call | flops 1 | bytes 1 | tf_op jit(solution)/shard_map/pallas_call | solution.py:250
  (2 shorter events, 0.0 us)
Async XLA Ops:
  0.6 0.8 %copy-start.1 = (bf16[256,128]{1,0:T(8,128)(2,1)S(1)}, bf16[256,128]{1,0:T(8,128)(2,1)}, u32[]{:S(2)}) copy-start(bf16[256,128]{1,0:T(8,128)(2,1)} %cotangent.1) | copy-start | bytes 196612
  0.6 0.9 %copy-start = (bf16[256,128]{1,0:T(8,128)(2,1)S(1)}, bf16[256,128]{1,0:T(8,128)(2,1)}, u32[]{:S(2)}) copy-start(bf16[256,128]{1,0:T(8,128)(2,1)} %hidden.1) | copy-start | bytes 196612
  0.7 0.9 %copy-start.4 = (s32[256]{0:T(256)S(1)}, s32[256]{0:T(256)}, u32[]{:S(2)}) copy-start(s32[256]{0:T(256)} %ids.1) | copy-start | bytes 3076
  0.7 0.8 %copy-start.3 = (bf16[12,128]{1,0:T(8,128)(2,1)S(1)}, bf16[12,128]{1,0:T(8,128)(2,1)}, u32[]{:S(2)}) copy-start(bf16[12,128]{1,0:T(8,128)(2,1)} %table.1) | copy-start | bytes 9220
  1.7 6.3 %collective-permute-start.1 = (bf16[2,256,128]{2,1,0:T(8,128)(2,1)S(1)}, bf16[2,256,128]{2,1,0:T(8,128)(2,1)S(1)}, u32[]{:S(2)}, u32[]{:S(2)}) collective-permute-start(bf16[2,256,128]{2,1,0:T(8,128)(2,1)S(1)} %shard_map.86.both), channel_id=1, source_target_pairs={{32,0},{64,32},{96,64},{128,96},{160,128},{192,160},{224,192},{256... | collective-permute-start | bytes 393224 | tf_op jit(solution)/shard_map/ppermute | solution.py:212
  3.0 21.5 %collective-permute-start = (bf16[2,256,128]{2,1,0:T(8,128)(2,1)S(1)}, bf16[2,256,128]{2,1,0:T(8,128)(2,1)S(1)}, u32[]{:S(2)}, u32[]{:S(2)}) collective-permute-start(bf16[2,256,128]{2,1,0:T(8,128)(2,1)S(1)} %shard_map.86.both), channel_id=1, source_target_pairs={{0,32},{32,64},{64,96},{96,128},{128,160},{160,192},{192,224},{224... | collective-permute-start | bytes 393224 | tf_op jit(solution)/shard_map/ppermute | solution.py:211
  9.2 15.4 %copy-start.2 = (bf16[16,256]{1,0:T(8,128)(2,1)S(1)}, bf16[16,256]{1,0:T(8,128)(2,1)}, u32[]{:S(2)}) copy-start(bf16[16,256]{1,0:T(8,128)(2,1)} %filters.1) | copy-start | bytes 24580
  9.2 15.4 %copy-start.5 = (s32[16]{0:T(128)S(1)}, s32[16]{0:T(128)}, u32[]{:S(2)}) copy-start(s32[16]{0:T(128)} %lengths.1) | copy-start | bytes 196
  9.2 17.9 %all-to-all-start = ((f32[16,4,128]{2,1,0:T(4,128)}), f32[16,4,128]{2,1,0:T(4,128)S(1)}, u32[]{:S(2)}, u32[]{:S(2)}) async-start(f32[16,4,128]{2,1,0:T(4,128)} %shard_map.89), calls=%async_computation | async-start | bytes 65536 | tf_op jit(solution)/shard_map/all_to_all | solution.py:230
